TPU v7x, 512 devices: a whole 4x8x8 slice. The times are simulated.
512 devices in a mesh: space: 64 (over y, z_lo, core), sample: 8 (over z_hi, x).
Axes of the slice: x: 4, y: 8, z: 8 (z_hi: 2, z_lo: 4; z = z_hi * 4 + z_lo), core: 2. Of those that a mesh axis runs over, the one named last changes fastest.
Arguments:
- volume: bfloat16 [8, 64, 32, 2048], P('sample', 'space'), may hold values from -6 to 6
- weight: bfloat16 [3, 3, 3, 64, 128], replicated, may hold values from -0.15625 to 0.15625
- conv_bias: float32 [128], replicated, may hold values from -3 to 3
- cotangent: bfloat16 [8, 512, 16, 128], P('sample', 'space'), may hold values from -6 to 6
Outputs:
- pooled: bfloat16 [8, 512, 16, 128], P('sample', 'space')
- input_grad: bfloat16 [8, 64, 32, 2048], P('sample', 'space')
- weight_grad: float32 [3, 3, 3, 64, 128], replicated
- bias_grad: float32 [128], replicated
All inputs are finite; a program needn't handle non-finite values.
Results may differ from a plain program's by a relative error of at most 0.013.
Values may be sent and summed in bfloat16 or wider, within the bound.
A program may use at most 64 MiB of HBM per device.

v0:
```python
import jax
import jax.numpy as jnp
from jax import lax
from jax.sharding import PartitionSpec as P

loss_scale = 256.0


def extended(value, sides, width):
    for axis, dim in sides:
        size, length = (lax.axis_size(axis), value.shape[dim])
        up = [(i, (i + 1) % size) for i in range(size - 1)]
        down = [(j, i) for i, j in up]
        last = lax.slice_in_dim(value, length - width, length, axis=dim)
        first = lax.slice_in_dim(value, 0, width, axis=dim)
        before = lax.ppermute(last, axis, up)
        after = lax.ppermute(first, axis, down)
        value = jnp.concatenate([before, value, after], axis=dim)
    return value


def partner(value, axis, bit):
    mask = 2**bit
    pairs = [(source, source ^ mask) for source in range(lax.axis_size(axis))]
    return lax.ppermute(value, axis, pairs)


def back_taps(grad_plane, weight_tap):
    flipped = jnp.transpose(weight_tap[::-1, ::-1], (0, 1, 3, 2))
    result = lax.conv_general_dilated(
        grad_plane[None],
        flipped,
        (1, 1),
        ((1, 1), (1, 1)),
        dimension_numbers=("NHWC", "HWIO", "NHWC"),
        preferred_element_type=jnp.float32,
    )
    return lax.optimization_barrier(result[0].astype(jnp.bfloat16))


def local(volume, weight, conv_bias, cotangent):
    side_cells = volume.shape[2]
    chan_in = weight.shape[3]
    chan_out = weight.shape[4]
    half_cells = side_cells // 2
    quarter_rows = side_cells // 4
    planes = extended(volume, (("space", 1),), 1)
    near_cells = planes.reshape(1, 3, side_cells, side_cells, chan_in)
    conv_out = lax.conv_general_dilated(
        near_cells,
        weight,
        (1, 1, 1),
        ((0, 0), (1, 1), (1, 1)),
        dimension_numbers=("NDHWC", "DHWIO", "NDHWC"),
        preferred_element_type=jnp.float32,
    )
    pre_act = conv_out[0, 0] + conv_bias
    sigmoid_pre = jax.nn.sigmoid(pre_act)
    activation = pre_act * sigmoid_pre
    windows = activation.reshape(half_cells, 2, half_cells, 2, chan_out)
    exp_act = jnp.exp(windows)
    numerator = jnp.sum(exp_act * windows, axis=(1, 3))
    denominator = jnp.sum(exp_act, axis=(1, 3))
    parity = lax.axis_index("space") % 2
    partner_half = 1 - parity

    def rows_of(table, which):
        return lax.dynamic_slice_in_dim(table, which * quarter_rows, quarter_rows, 0)

    def whole_rows(mine, theirs):
        table = jnp.zeros((half_cells, half_cells, chan_out), jnp.float32)
        table = lax.dynamic_update_slice_in_dim(table, mine, parity * quarter_rows, 0)
        return lax.dynamic_update_slice_in_dim(table, theirs, partner_half * quarter_rows, 0)

    upstream = cotangent[0].astype(jnp.float32)
    got_num, got_den = partner(
        (rows_of(numerator, partner_half), rows_of(denominator, partner_half)), "space", 0
    )
    total_den = rows_of(denominator, parity) + got_den
    pool_value = (rows_of(numerator, parity) + got_num) / total_den
    pooled = pool_value.astype(jnp.bfloat16)[None]
    coef_b = upstream / total_den
    coef_a = coef_b * (1.0 - pool_value)
    far_a, far_b = partner((coef_a, coef_b), "space", 0)
    full_a = whole_rows(coef_a, far_a)[:, None, :, None, :]
    full_b = whole_rows(coef_b, far_b)[:, None, :, None, :]
    grad_act = (exp_act * (full_a + full_b * windows)).reshape(side_cells, side_cells, chan_out)
    grad_pre = (grad_act * sigmoid_pre * (1.0 + pre_act * (1.0 - sigmoid_pre))).astype(jnp.bfloat16)
    grad_pre = lax.optimization_barrier(grad_pre)
    bias_part = jnp.sum(grad_pre.astype(jnp.float32), axis=(0, 1))
    padded = jnp.pad(near_cells[0], ((0, 0), (1, 1), (1, 1), (0, 0)))
    flat_grad = grad_pre.reshape(side_cells * side_cells, chan_out)
    tap_list = []
    for depth_tap in range(3):
        for row_tap in range(3):
            for col_tap in range(3):
                window = padded[
                    depth_tap, row_tap : row_tap + side_cells, col_tap : col_tap + side_cells
                ].reshape(side_cells * side_cells, chan_in)
                tap_list.append(
                    lax.dot_general(
                        window,
                        flat_grad,
                        (((0,), (0,)), ((), ())),
                        preferred_element_type=jnp.float32,
                    )
                )
    weight_part = jnp.stack(tap_list).reshape(3, 3, 3, chan_in, chan_out)
    weight_total, bias_total = lax.psum((weight_part, bias_part), ("space", "sample"))
    weight_grad = weight_total / loss_scale
    bias_grad = bias_total / loss_scale
    grad_rows = grad_pre.reshape(1, 1, side_cells, side_cells * chan_out)
    grad_near = extended(grad_rows, (("space", 1),), 1)
    grad_near = grad_near.reshape(3, side_cells, side_cells, chan_out)
    term_upper = back_taps(grad_near[2], weight[0])
    term_middle = back_taps(grad_near[1], weight[1])
    term_lower = back_taps(grad_near[0], weight[2])
    summed = (
        term_upper.astype(jnp.float32)
        + term_middle.astype(jnp.float32)
        + term_lower.astype(jnp.float32)
    )
    summed = summed.reshape(side_cells, side_cells * chan_in)
    input_grad = summed.astype(jnp.bfloat16).reshape(1, 1, side_cells, side_cells * chan_in)
    return (pooled, input_grad, weight_grad, bias_grad)


def solution(mesh):
    placed = (P("sample", "space", None, None), P(), P(), P("sample", "space", None, None))
    return jax.shard_map(
        local,
        mesh=mesh,
        in_specs=placed,
        out_specs=(P("sample", "space", None, None), P("sample", "space", None, None), P(), P()),
        check_vma=False,
    )
```

profile of v0, /device:TPU:1, one launch (start us, length us, event | category | flops | bytes accessed | tf_op | source)
XLA Modules:
  0.0 347.3 jit_solution(12180079642724064991)
XLA Ops:
  7.2 5.4 %collective-permute-start = (bf16[1,1,32,2048]{3,2,1,0:T(8,128)(2,1)}, bf16[1,1,32,2048]{3,2,1,0:T(8,128)(2,1)S(1)}, u32[]{:S(2)}, u32[]{:S(2)}) collective-permute-start(bf16[1,1,32,2048]{3,2,1,0:T(8,128)(2,1)} %param.4), channel_id=1, source_target_pairs={{0,8},{8,16},{16,24},{24,32},{32,40},{40,48},{48,56},{56,64},{64,7... | collective-permute-start | bytes 393224 | tf_op jit(solution)/shard_map/ppermute | solution.py:16
  12.6 4.7 %collective-permute-start.1 = (bf16[1,1,32,2048]{3,2,1,0:T(8,128)(2,1)}, bf16[1,1,32,2048]{3,2,1,0:T(8,128)(2,1)S(1)}, u32[]{:S(2)}, u32[]{:S(2)}) collective-permute-start(bf16[1,1,32,2048]{3,2,1,0:T(8,128)(2,1)} %param.4), channel_id=1, source_target_pairs={{8,0},{16,8},{24,16},{32,24},{40,32},{48,40},{56,48},{64,56},{72,6... | collective-permute-start | bytes 393224 | tf_op jit(solution)/shard_map/ppermute | solution.py:17
  17.3 1.9 reshape_squeeze.94
  19.3 0.9 constant_dynamic-update-slice_fusion.1
  20.2 0.8 reshape.109
  21.0 0.8 squeeze_reshape.3
  21.8 1.3 pad_slice_fusion.1
  23.1 2.5 pad_slice_fusion
  26.7 0.5 copy-done.25
  27.2 1.5 fusion.11
  28.8 0.5 copy-done.24
  29.8 1.9 collective-permute-start.3
  31.8 2.4 collective-permute-start.2
  34.2 1.0 reshape_squeeze.85
  35.1 1.0 reshape_squeeze.103
  36.2 1.9 collective-permute-start.5
  38.2 2.4 collective-permute-start.4
  40.6 0.6 copy.111
  42.6 2.4 collective-permute-start.6
  45.0 3.5 %collective-permute-start.7 = (bf16[1,1,32,4096]{3,2,1,0:T(8,128)(2,1)S(1)}, bf16[1,1,32,4096]{3,2,1,0:T(8,128)(2,1)}, u32[]{:S(2)}, u32[]{:S(2)}) collective-permute-start(bf16[1,1,32,4096]{3,2,1,0:T(8,128)(2,1)S(1)} %reshape.77), channel_id=1, source_target_pairs={{0,8},{8,16},{16,24},{24,32},{32,40},{40,48},{48,56},{56,64},{64,7... | collective-permute-start | bytes 786440 | tf_op jit(solution)/shard_map/ppermute | solution.py:16
  55.6 0.9 copy-done.20
  56.8 0.8 copy-done.26
  57.5 0.9 fusion.9
  58.5 112.0 %psum.15 = f32[128]{0:T(128)S(1)} all-reduce(f32[128]{0:T(128)S(1)} %convert_reduce_fusion), channel_id=1, replica_groups=mesh['space'=64,'sample'=8] {'space','sample'}, use_global_device_ids=true, to_apply=%region_4.5 | all-reduce | flops 128 | bytes 1024 | tf_op jit(solution)/shard_map/psum | solution.py:109
  170.6 0.5 broadcast_multiply_fusion.1
  171.1 1.0 copy.123
  172.4 0.9 fusion.8
  173.4 1.0 copy.124
  174.8 0.9 fusion.10
  176.0 0.9 convert_element_type.71
  176.9 161.3 %all-reduce.3.cloned.1.call-done = f32[3,3,3,64,128]{4,3,2,1,0:T(8,128)} async-done(((f32[3,3,3,64,128]{4,3,2,1,0:T(8,128)}), f32[3,3,3,64,128]{4,3,2,1,0:T(8,128)}) %all-reduce.3.cloned.1.call-update) | async-done | bytes 884752 | tf_op jit(solution)/shard_map/psum | solution.py:109
  338.3 2.2 broadcast_multiply_fusion
  (133 shorter events, 11.0 us)
Async XLA Ops:
  7.2 331.1 %all-reduce.3.cloned.1.call-start = ((), (), s32[]{:S(2)}) async-start(), calls=%async_computation | async-start | bytes 1769472 | tf_op jit(solution)/shard_map/psum | solution.py:109
  7.2 12.0 %collective-permute-start = (bf16[1,1,32,2048]{3,2,1,0:T(8,128)(2,1)}, bf16[1,1,32,2048]{3,2,1,0:T(8,128)(2,1)S(1)}, u32[]{:S(2)}, u32[]{:S(2)}) collective-permute-start(bf16[1,1,32,2048]{3,2,1,0:T(8,128)(2,1)} %param.4), channel_id=1, source_target_pairs={{0,8},{8,16},{16,24},{24,32},{32,40},{40,48},{48,56},{56,64},{64,7... | collective-permute-start | bytes 393224 | tf_op jit(solution)/shard_map/ppermute | solution.py:16
  12.6 7.6 %collective-permute-start.1 = (bf16[1,1,32,2048]{3,2,1,0:T(8,128)(2,1)}, bf16[1,1,32,2048]{3,2,1,0:T(8,128)(2,1)S(1)}, u32[]{:S(2)}, u32[]{:S(2)}) collective-permute-start(bf16[1,1,32,2048]{3,2,1,0:T(8,128)(2,1)} %param.4), channel_id=1, source_target_pairs={{8,0},{16,8},{24,16},{32,24},{40,32},{48,40},{56,48},{64,56},{72,6... | collective-permute-start | bytes 393224 | tf_op jit(solution)/shard_map/ppermute | solution.py:17
  20.2 1.6 copy-start.21
  26.1 1.0 copy-start.25
  29.3 5.9 %copy-start.22 = (bf16[1,1,32,2048]{3,2,1,0:T(8,128)(2,1)S(1)}, bf16[1,1,32,2048]{3,2,1,0:T(8,128)(2,1)}, u32[]{:S(2)}) copy-start(bf16[1,1,32,2048]{3,2,1,0:T(8,128)(2,1)} %copy-done.21) | copy-start | bytes 393220
  29.7 6.4 %copy-start.23 = (bf16[1,8,16,128]{3,2,1,0:T(8,128)(2,1)S(1)}, bf16[1,8,16,128]{3,2,1,0:T(8,128)(2,1)}, u32[]{:S(2)}) copy-start(bf16[1,8,16,128]{3,2,1,0:T(8,128)(2,1)} %param.7) | copy-start | bytes 98308
  29.8 6.3 %collective-permute-start.3 = (f32[8,16,128]{2,0,1:T(8,128)S(1)}, f32[8,16,128]{2,0,1:T(8,128)S(1)}, u32[]{:S(2)}, u32[]{:S(2)}) collective-permute-start(f32[8,16,128]{2,0,1:T(8,128)S(1)} %copy.119), channel_id=1, source_target_pairs={{0,8},{8,0},{16,24},{24,16},{32,40},{40,32},{48,56},{56,48},{64,72... | collective-permute-start | bytes 196616 | tf_op jit(solution)/shard_map/ppermute | solution.py:25
  31.8 6.3 %collective-permute-start.2 = (f32[8,16,128]{2,0,1:T(8,128)S(1)}, f32[8,16,128]{2,0,1:T(8,128)S(1)}, u32[]{:S(2)}, u32[]{:S(2)}) collective-permute-start(f32[8,16,128]{2,0,1:T(8,128)S(1)} %copy.117), channel_id=1, source_target_pairs={{0,8},{8,0},{16,24},{24,16},{32,40},{40,32},{48,56},{56,48},{64,72... | collective-permute-start | bytes 196616 | tf_op jit(solution)/shard_map/ppermute | solution.py:25
  36.2 5.1 %collective-permute-start.5 = (f32[8,16,128]{2,0,1:T(8,128)S(1)}, f32[8,16,128]{2,0,1:T(8,128)S(1)}, u32[]{:S(2)}, u32[]{:S(2)}) collective-permute-start(f32[8,16,128]{2,0,1:T(8,128)S(1)} %get-tuple-element.19), channel_id=1, source_target_pairs={{0,8},{8,0},{16,24},{24,16},{32,40},{40,32},{48,56},{56,48},{64,72... | collective-permute-start | bytes 196616 | tf_op jit(solution)/shard_map/ppermute | solution.py:25
  38.2 3.3 collective-permute-start.4
  42.3 6.3 %copy-start.19 = (bf16[1,32,32,64]{3,2,1,0:T(8,128)(2,1)S(1)}, bf16[1,32,32,64]{3,2,1,0:T(8,128)(2,1)}, u32[]{:S(2)}) copy-start(bf16[1,32,32,64]{3,2,1,0:T(8,128)(2,1)} %get-tuple-element.46) | copy-start | bytes 393220
  42.3 6.6 %copy-start.11 = (bf16[1,32,32,64]{3,2,1,0:T(8,128)(2,1)S(1)}, bf16[1,32,32,64]{3,2,1,0:T(8,128)(2,1)}, u32[]{:S(2)}) copy-start(bf16[1,32,32,64]{3,2,1,0:T(8,128)(2,1)} %get-tuple-element.24) | copy-start | bytes 393220
  42.5 6.7 %copy-start.10 = (bf16[1,32,32,64]{3,2,1,0:T(8,128)(2,1)S(1)}, bf16[1,32,32,64]{3,2,1,0:T(8,128)(2,1)}, u32[]{:S(2)}) copy-start(bf16[1,32,32,64]{3,2,1,0:T(8,128)(2,1)} %get-tuple-element.25) | copy-start | bytes 393220
  42.6 6.8 %copy-start.9 = (bf16[1,32,32,64]{3,2,1,0:T(8,128)(2,1)S(1)}, bf16[1,32,32,64]{3,2,1,0:T(8,128)(2,1)}, u32[]{:S(2)}) copy-start(bf16[1,32,32,64]{3,2,1,0:T(8,128)(2,1)} %get-tuple-element.26) | copy-start | bytes 393220
  42.6 128.5 %collective-permute-start.6 = (bf16[1,1,32,4096]{3,2,1,0:T(8,128)(2,1)S(1)}, bf16[1,1,32,4096]{3,2,1,0:T(8,128)(2,1)}, u32[]{:S(2)}, u32[]{:S(2)}) collective-permute-start(bf16[1,1,32,4096]{3,2,1,0:T(8,128)(2,1)S(1)} %reshape.77), channel_id=1, source_target_pairs={{8,0},{16,8},{24,16},{32,24},{40,32},{48,40},{56,48},{64,56},{72,6... | collective-permute-start | bytes 786440 | tf_op jit(solution)/shard_map/ppermute | solution.py:17
  45.0 128.4 %collective-permute-start.7 = (bf16[1,1,32,4096]{3,2,1,0:T(8,128)(2,1)S(1)}, bf16[1,1,32,4096]{3,2,1,0:T(8,128)(2,1)}, u32[]{:S(2)}, u32[]{:S(2)}) collective-permute-start(bf16[1,1,32,4096]{3,2,1,0:T(8,128)(2,1)S(1)} %reshape.77), channel_id=1, source_target_pairs={{0,8},{8,16},{16,24},{24,32},{32,40},{40,48},{48,56},{56,64},{64,7... | collective-permute-start | bytes 786440 | tf_op jit(solution)/shard_map/ppermute | solution.py:16
  48.6 1.0 copy-start.14
  48.9 1.1 copy-start.8
  49.2 1.1 copy-start.7
  49.4 1.1 copy-start.6
  49.7 1.1 copy-start.5
  50.0 1.1 copy-start.4
  50.2 1.1 copy-start.3
  50.5 1.1 copy-start.2
  50.8 1.1 copy-start.1
  51.0 1.0 copy-start.12
  51.3 1.0 copy-start
  53.3 1.0 copy-start.13
  53.6 1.0 copy-start.17
  53.8 1.0 copy-start.16
  56.5 1.0 copy-start.26
  (5 other events, 4.6 us)
Sparse Core Ops, SparseCore 0:
  56.7 281.5 all-reduce.2
where the time goes:
time: 348 us; the launch traced here: 347 us
  waiting for transfers between devices  162 us (47%)
  blocking collectives  112 us (32%)
  starting transfers between devices  24.7 us (7%)
  local copies, waits for them, and re-layouts  19.5 us (6%)
  between operations  15.1 us (4%)
  matrix products  10.6 us (3%)
  other arithmetic  3.78 us (1%)
    psum x1, waiting for transfers between devices, local(): lax.psum((weight_part, bias_part), ('space', 'sample'))  161 us
    psum x1, blocking collectives, local(): lax.psum((weight_part, bias_part), ('space', 'sample'))  112 us
    ppermute x2, starting transfers between devices, extended(): before = lax.ppermute(last, axis, up)  8.87 us
    ppermute x4, starting transfers between devices, partner(): return lax.ppermute(value, axis, pairs)  8.65 us
    ppermute x2, starting transfers between devices, extended(): after = lax.ppermute(first, axis, down)  7.09 us
  transfers between devices with their start and end apart: 9, of which 2 were waited for; matrix products, arithmetic and copies ran while one was open for 6% of the time, Pallas kernels for 0%

commit v1 on v0

--- a/solution.py
+++ b/solution.py
@@ -1,7 +1,205 @@
 import jax
 import jax.numpy as jnp
 from jax import lax
+from jax.experimental import pallas as pl
+from jax.experimental.pallas import tpu as pltpu
 from jax.sharding import PartitionSpec as P
+
+MESH = pl.DeviceIdType.MESH
+BF16 = jnp.bfloat16
+F32 = jnp.float32
+taps = 27
+pieces = 28
+per_kind = 14
+ring_order = (4, 3, 5, 2, 6, 1, 7)
+plane_order = sorted(
+    [(dx, dr) for dx in range(4) for dr in range(8) if (dx, dr) != (0, 0)],
+    key=lambda d: -(min(d[0], 4 - d[0]) + min(d[1], 8 - d[1])),
+)
+
+
+def place():
+    space = lax.axis_index("space")
+    sample = lax.axis_index("sample")
+    core = lax.rem(space, 2)
+    z_lo = lax.rem(lax.div(space, 2), 4)
+    y = lax.div(space, 8)
+    z = lax.div(sample, 4) * 4 + z_lo
+    x = lax.rem(sample, 4)
+    return x, y, z, core
+
+
+def ident(x, y, z, core):
+    return ((y * 4 + lax.rem(z, 4)) * 2 + core, lax.div(z, 4) * 4 + x)
+
+
+class Reduce:
+    def __init__(self):
+        self.x, self.y, self.z, self.core = place()
+        x, y, z = self.x, self.y, self.z
+        self.kind_a = x < 2
+        self.ring_at = jnp.where(self.kind_a, z, y)
+        self.row_at = jnp.where(self.kind_a, y, z)
+        spot = lax.rem(x, 2) * 8 + self.row_at
+        self.owner = spot < per_kind
+        self.kind = jnp.where(self.kind_a, 0, 1)
+        self.piece = jnp.minimum(self.kind * per_kind + spot, pieces - 1)
+        self.slot = x * 8 + self.row_at
+        self.partner = ident(x, y, z, 1 - self.core)
+
+    def plane_peer(self, dx, dr):
+        row = lax.rem(self.row_at + dr, 8)
+        y = jnp.where(self.kind_a, row, self.y)
+        z = jnp.where(self.kind_a, self.z, row)
+        return ident(lax.rem(self.x + dx, 4), y, z, self.core)
+
+    def ring_peer(self, dr):
+        at = lax.rem(self.ring_at + dr, 8)
+        y = jnp.where(self.kind_a, self.y, at)
+        z = jnp.where(self.kind_a, at, self.z)
+        return ident(self.x, y, z, self.core)
+
+    def owner_of(self, piece):
+        kind, spot = divmod(piece, per_kind)
+        x = 2 * kind + spot // 8
+        row = spot % 8
+        if kind == 0:
+            return ident(x, row, self.z, self.core), self.x * 8 + self.y
+        return ident(x, self.y, row, self.core), self.x * 8 + self.z
+
+
+def signal(sem, who):
+    pl.semaphore_signal(sem, inc=1, device_id=who, device_id_type=MESH)
+
+
+def remote(src, dst, send, recv, who):
+    return pltpu.make_async_remote_copy(
+        src_ref=src, dst_ref=dst, send_sem=send, recv_sem=recv, device_id=who, device_id_type=MESH
+    )
+
+
+def reduce_kernel(
+    part_ref, total_ref, mine, theirs, rows, rs, ring_src, ring, final, gath,
+    core_send, core_recv, rs_send, rs_recv, ring_send, ring_recv, ag_send, ag_recv, fw_send, fw_recv,
+):
+    r = Reduce()
+    bar = pltpu.get_barrier_semaphore()
+
+    @pl.when(r.owner)
+    def _():
+        for dx, dr in plane_order:
+            signal(bar, r.plane_peer(dx, dr))
+        for dr in ring_order:
+            signal(bar, r.ring_peer(dr))
+
+    signal(bar, r.partner)
+    own = jnp.where(r.owner, 1, 0)
+    pl.semaphore_wait(bar, pieces + 1 + 6 * own)
+
+    half = r.core * 32
+    far_half = 32 - half
+    core_copies = []
+    for g in range(4):
+        span = pl.ds(7 * g, 7)
+        mine[span] = part_ref[span, pl.ds(pl.multiple_of(far_half, 32), 32), :].astype(BF16)
+        cp = remote(mine.at[span], theirs.at[span], core_send.at[g], core_recv.at[g], r.partner)
+        cp.start()
+        core_copies.append(cp)
+    rs_copies = []
+    for g in range(4):
+        span = pl.ds(7 * g, 7)
+        core_copies[g].wait_recv()
+        rows[span] = (
+            part_ref[span, pl.ds(pl.multiple_of(half, 32), 32), :] + theirs[span].astype(F32)
+        ).astype(BF16)
+        for piece in range(7 * g, 7 * g + 7):
+            who, slot = r.owner_of(piece)
+            is_me = jnp.logical_and(r.owner, r.piece == piece)
+            cp = remote(rows.at[piece], rs.at[slot], rs_send.at[piece], rs_recv, who)
+            rs_copies.append((is_me, cp))
+
+            @pl.when(jnp.logical_not(is_me))
+            def _(cp=cp):
+                cp.start()
+
+            @pl.when(is_me)
+            def _(piece=piece):
+                pltpu.make_async_copy(rows.at[piece], rs.at[r.slot], rs_recv).start()
+
+    @pl.when(r.owner)
+    def _():
+        pltpu.make_async_copy(rs, rs, rs_recv).wait()
+        total = rs[0].astype(F32)
+        for i in range(1, 32):
+            total = total + rs[i].astype(F32)
+        ring_src[...] = total.astype(BF16)
+        copies = []
+        for dr in ring_order:
+            cp = remote(ring_src, ring.at[r.ring_at], ring_send.at[dr], ring_recv, r.ring_peer(dr))
+            cp.start()
+            copies.append(cp)
+        pltpu.make_async_copy(ring_src, ring.at[r.ring_at], ring_recv).start()
+        pltpu.make_async_copy(ring, ring, ring_recv).wait()
+        total = ring[0].astype(F32)
+        for i in range(1, 8):
+            total = total + ring[i].astype(F32)
+        final[...] = total.astype(BF16)
+        for i, (dx, dr) in enumerate(plane_order):
+            cp = remote(
+                final, gath.at[r.core, r.piece], ag_send.at[i], ag_recv.at[r.kind], r.plane_peer(dx, dr)
+            )
+            cp.start()
+            copies.append(cp)
+        pltpu.make_async_copy(final, gath.at[r.core, r.piece], ag_recv.at[r.kind]).start()
+        for cp in copies:
+            cp.wait_send()
+
+    fw_copies = []
+    for kind in range(2):
+        span = gath.at[r.core, pl.ds(per_kind * kind, per_kind)]
+        pltpu.make_async_copy(span, span, ag_recv.at[kind]).wait()
+        cp = remote(span, span, fw_send.at[kind], fw_recv.at[kind], r.partner)
+        cp.start()
+        fw_copies.append(cp)
+    for cp in core_copies:
+        cp.wait_send()
+    for is_me, cp in rs_copies:
+
+        @pl.when(jnp.logical_not(is_me))
+        def _(cp=cp):
+            cp.wait_send()
+
+    for cp in fw_copies:
+        cp.wait()
+    scale = 1.0 / loss_scale
+    for h in range(2):
+        total_ref[:, 32 * h : 32 * h + 32, :] = gath[h].astype(F32) * scale
+
+
+def reduced(part):
+    dma = pltpu.SemaphoreType.DMA
+    return pl.pallas_call(
+        reduce_kernel,
+        out_shape=jax.ShapeDtypeStruct((pieces, 64, 128), F32),
+        in_specs=[pl.BlockSpec(memory_space=pltpu.VMEM)],
+        out_specs=pl.BlockSpec(memory_space=pltpu.VMEM),
+        scratch_shapes=[
+            pltpu.VMEM((pieces, 32, 128), BF16),
+            pltpu.VMEM((pieces, 32, 128), BF16),
+            pltpu.VMEM((pieces, 32, 128), BF16),
+            pltpu.VMEM((32, 32, 128), BF16),
+            pltpu.VMEM((32, 128), BF16),
+            pltpu.VMEM((8, 32, 128), BF16),
+            pltpu.VMEM((32, 128), BF16),
+            pltpu.VMEM((2, pieces, 32, 128), BF16),
+            dma((4,)), dma((4,)), dma((pieces,)), dma, dma((8,)), dma, dma((31,)), dma((2,)), dma((2,)), dma((2,)),
+        ],
+        compiler_params=pltpu.CompilerParams(
+            collective_id=0, has_side_effects=True, vmem_limit_bytes=32 * 2**20
+        ),
+        name="reduce_weight_grad",
+    )(part)
+
 
 loss_scale = 256.0
 
@@ -105,10 +303,11 @@
                         preferred_element_type=jnp.float32,
                     )
                 )
-    weight_part = jnp.stack(tap_list).reshape(3, 3, 3, chan_in, chan_out)
-    weight_total, bias_total = lax.psum((weight_part, bias_part), ("space", "sample"))
-    weight_grad = weight_total / loss_scale
-    bias_grad = bias_total / loss_scale
+    bias_block = jnp.pad(bias_part[None, None], ((0, 0), (0, chan_in - 1), (0, 0)))
+    part = jnp.concatenate([jnp.stack(tap_list), bias_block], axis=0)
+    total = reduced(part)
+    weight_grad = total[:taps].reshape(3, 3, 3, chan_in, chan_out)
+    bias_grad = total[taps, 0]
     grad_rows = grad_pre.reshape(1, 1, side_cells, side_cells * chan_out)
     grad_near = extended(grad_rows, (("space", 1),), 1)
     grad_near = grad_near.reshape(3, side_cells, side_cells, chan_out)

time: 348 us -> 102 us (0.29)
  waiting for transfers between devices: 162 us -> 0.87 us
  blocking collectives: 112 us -> 0 us
  Pallas kernels: 0 us -> 42.3 us
  between operations: 15.1 us -> 1.69 us
  matrix products: 10.6 us -> 14.7 us
  local copies, waits for them, and re-layouts: 19.5 us -> 15.6 us
    psum x1 -> x0, waiting for transfers between devices: 161 us -> none  [local(): lax.psum((weight_part, bias_part), ('space', 'sample'))]
    psum x1 -> x0, blocking collectives: 112 us -> none  [local(): lax.psum((weight_part, bias_part), ('space', 'sample'))]
    pallas_call x0 -> x1, Pallas kernels: none -> 42.3 us  [reduced(): pl.pallas_call(reduce_kernel, out_shape=jax.ShapeDtypeStruct((pieces, 64,...]
    unnamed x66 -> x67, local copies, waits for them, and re-layouts: 6.84 us -> 2.8 us
  transfers between devices with their start and end apart: 9 -> 8, of which waited for: 2 -> 1; matrix products, arithmetic and copies ran while one was open for 6% -> 15% of each run, Pallas kernels for 0% -> 42%
where the time goes in v1:
time: 102 us; the launch traced here: 101 us
  Pallas kernels  42.3 us (41%)
  starting transfers between devices  24.5 us (24%)
  local copies, waits for them, and re-layouts  15.6 us (15%)
  matrix products  14.7 us (14%)
  between operations  1.69 us (2%)
  other arithmetic  1.5 us (1%)
    pallas_call x1, Pallas kernels, reduced(): pl.pallas_call(reduce_kernel, out_shape=jax.ShapeDtypeStruct((pieces, 64,...  42.3 us
    ppermute x2, starting transfers between devices, extended(): before = lax.ppermute(last, axis, up)  8.87 us
    ppermute x4, starting transfers between devices, partner(): return lax.ppermute(value, axis, pairs)  8.64 us
    ppermute x2, starting transfers between devices, extended(): after = lax.ppermute(first, axis, down)  6.95 us
    dot_general x27, matrix products, local(): lax.dot_general(window, flat_grad, (((0,), (0,)), ((), ())), preferred_el...  6.33 us
    conv_general_dilated x1, matrix products, local(): lax.conv_general_dilated(near_cells, weight, (1, 1, 1), ((0, 0), (1, 1),...  4.68 us
    slice x2, local copies, waits for them, and re-layouts, local(): padded[depth_tap, row_tap:row_tap + side_cells, col_tap:col_tap + side_ce...  3.85 us
    conv_general_dilated x3, matrix products, back_taps(): lax.conv_general_dilated(grad_plane[None], flipped, (1, 1), ((1, 1), (1,...  3.7 us
  transfers between devices with their start and end apart: 8, of which 1 were waited for; matrix products, arithmetic and copies ran while one was open for 15% of the time, Pallas kernels for 42%

profile of v1, /device:TPU:1, one launch (start us, length us, event | category | flops | bytes accessed | tf_op | source)
XLA Modules:
  0.0 101.1 jit_solution(1166853405756846889)
XLA Ops:
  0.6 5.4 %collective-permute-start = (bf16[1,1,32,2048]{3,2,1,0:T(8,128)(2,1)}, bf16[1,1,32,2048]{3,2,1,0:T(8,128)(2,1)S(1)}, u32[]{:S(2)}, u32[]{:S(2)}) collective-permute-start(bf16[1,1,32,2048]{3,2,1,0:T(8,128)(2,1)} %param.4), channel_id=1, source_target_pairs={{0,8},{8,16},{16,24},{24,32},{32,40},{40,48},{48,56},{56,64},{64,7... | collective-permute-start | bytes 393224 | tf_op jit(solution)/shard_map/ppermute | solution.py:214
  6.0 4.7 %collective-permute-start.1 = (bf16[1,1,32,2048]{3,2,1,0:T(8,128)(2,1)}, bf16[1,1,32,2048]{3,2,1,0:T(8,128)(2,1)S(1)}, u32[]{:S(2)}, u32[]{:S(2)}) collective-permute-start(bf16[1,1,32,2048]{3,2,1,0:T(8,128)(2,1)} %param.4), channel_id=1, source_target_pairs={{8,0},{16,8},{24,16},{32,24},{40,32},{48,40},{56,48},{64,56},{72,6... | collective-permute-start | bytes 393224 | tf_op jit(solution)/shard_map/ppermute | solution.py:215
  10.8 1.9 %reshape_squeeze.94 = bf16[1024,64]{1,0:T(8,128)(2,1)} reshape(bf16[1,1,32,2048]{3,2,1,0:T(8,128)(2,1)} %param.4) | data formatting | bytes 262144 | tf_op jit(solution)/shard_map/reshape;squeeze | solution.py:297
  12.7 1.0 constant_dynamic-update-slice_fusion.1
  13.7 0.6 copy-done.23
  14.3 1.1 %reshape.123 = bf16[1,3,32,32,64]{4,0,3,2,1:T(2,128)(2,1)S(1)} reshape(bf16[1,3,32,2048]{3,2,1,0:T(8,128)(2,1)S(1)} %constant_dynamic-update-slice_fusion) | data formatting | bytes 786432 | tf_op jit(solution)/shard_map/reshape | solution.py:246
  15.4 0.8 squeeze_reshape.3
  16.2 1.2 %pad_slice_fusion.1 = (bf16[1,32,32,64]{3,2,1,0:T(8,128)(2,1)}, bf16[1,32,32,64]{3,2,1,0:T(8,128)(2,1)}, bf16[1,32,32,64]{3,2,1,0:T(8,128)(2,1)}, bf16[1,32,32,64]{3,2,1,0:T(8,128)(2,1)}, bf16[1,32,32,64]{3,2,1,0:T(8,128)(2,1)}) fusion(bf16[3,32,32,64]{3,2,1,0:T(8,128)(2,1)S(1)} %squeeze_reshape.3), kind=kLoop, calls=%fused_computation.7 | loop fusion | bytes 1048576 | tf_op jit(solution)/shard_map/slice | solution.py:295
  17.5 2.6 %pad_slice_fusion = (bf16[1,32,32,64]{3,2,1,0:T(8,128)(2,1)S(1)}, bf16[1,32,32,64]{3,2,1,0:T(8,128)(2,1)}, bf16[1,32,32,64]{3,2,1,0:T(8,128)(2,1)}, bf16[1,32,32...) fusion(bf16[3,32,32,64]{3,2,1,0:T(8,128)(2,1)S(1)} %squeeze_res, ...), kind=kLoop, calls=%fused_computation.6 | loop fusion | bytes 2883584 | tf_op jit(solution)/shard_map/slice | solution.py:295
  20.1 4.7 %fusion.70 = f32[1,1,32,32,128]{4,0,3,2,1:T(1,128)S(1)} fusion(bf16[1,3,32,32,64]{4,0,3,2,1:T(2,128)(2,1)S(1)} %reshape.123, bf16[3,3,3,64,128]{4,3,2,1,0:T(8,128)(2,1)S(1)} %copy-done.27), kind=kOutput, calls=%fused_computation.148 | convolution fusion | flops 434307072 | bytes 1359872 | tf_op jit(solution)/shard_map/conv_general_dilated | solution.py:247
  24.8 0.2 exponential_reduce_fusion
  25.1 1.9 %collective-permute-start.3 = (f32[8,16,128]{2,1,0:T(8,128)S(1)}, f32[8,16,128]{2,1,0:T(8,128)S(1)}, u32[]{:S(2)}, u32[]{:S(2)}) collective-permute-start(f32[8,16,128]{2,1,0:T(8,128)S(1)} %constant_dynamic-slice_fusion), channel_id=1, source_target_pairs={{0,8},{8,0},{16,24},{24,16},{32,40},{40,32},{48,56},{56,48},{64,72... | collective-permute-start | bytes 196616 | tf_op jit(solution)/shard_map/ppermute | solution.py:223
  27.0 2.4 %collective-permute-start.2 = (f32[8,16,128]{2,1,0:T(8,128)S(1)}, f32[8,16,128]{2,1,0:T(8,128)S(1)}, u32[]{:S(2)}, u32[]{:S(2)}) collective-permute-start(f32[8,16,128]{2,1,0:T(8,128)S(1)} %constant_dynamic-slice_fusion.1), channel_id=1, source_target_pairs={{0,8},{8,0},{16,24},{24,16},{32,40},{40,32},{48,56},{56,48},{64,72... | collective-permute-start | bytes 196616 | tf_op jit(solution)/shard_map/ppermute | solution.py:223
  29.5 0.2 reshape_squeeze.85
  29.7 0.2 reshape_squeeze.103
  30.0 1.9 %collective-permute-start.5 = (f32[8,16,128]{2,1,0:T(8,128)S(1)}, f32[8,16,128]{2,1,0:T(8,128)S(1)}, u32[]{:S(2)}, u32[]{:S(2)}) collective-permute-start(f32[8,16,128]{2,1,0:T(8,128)S(1)} %get-tuple-element.7), channel_id=1, source_target_pairs={{0,8},{8,0},{16,24},{24,16},{32,40},{40,32},{48,56},{56,48},{64,72... | collective-permute-start | bytes 196616 | tf_op jit(solution)/shard_map/ppermute | solution.py:223
  32.0 0.6 constant_dynamic-update-slice_fusion.7
  32.6 2.4 %collective-permute-start.4 = (f32[8,16,128]{2,1,0:T(8,128)S(1)}, f32[8,16,128]{2,1,0:T(8,128)S(1)}, u32[]{:S(2)}, u32[]{:S(2)}) collective-permute-start(f32[8,16,128]{2,1,0:T(8,128)S(1)} %get-tuple-element.9), channel_id=1, source_target_pairs={{0,8},{8,0},{16,24},{24,16},{32,40},{40,32},{48,56},{56,48},{64,72... | collective-permute-start | bytes 196616 | tf_op jit(solution)/shard_map/ppermute | solution.py:223
  35.1 0.8 collective-permute-done.4
  36.2 0.2 add.97
  36.4 0.3 multiply_convert_fusion
  36.9 0.8 reshape.77
  37.7 2.3 %collective-permute-start.6 = (bf16[1,1,32,4096]{3,2,1,0:T(8,128)(2,1)}, bf16[1,1,32,4096]{3,2,1,0:T(8,128)(2,1)S(1)}, u32[]{:S(2)}, u32[]{:S(2)}) collective-permute-start(bf16[1,1,32,4096]{3,2,1,0:T(8,128)(2,1)} %reshape.77), channel_id=1, source_target_pairs={{8,0},{16,8},{24,16},{32,24},{40,32},{48,40},{56,48},{64,56},{72,6... | collective-permute-start | bytes 786440 | tf_op jit(solution)/shard_map/ppermute | solution.py:215
  40.0 3.5 %collective-permute-start.7 = (bf16[1,1,32,4096]{3,2,1,0:T(8,128)(2,1)}, bf16[1,1,32,4096]{3,2,1,0:T(8,128)(2,1)S(1)}, u32[]{:S(2)}, u32[]{:S(2)}) collective-permute-start(bf16[1,1,32,4096]{3,2,1,0:T(8,128)(2,1)} %reshape.77), channel_id=1, source_target_pairs={{0,8},{8,16},{16,24},{24,32},{32,40},{40,48},{48,56},{56,64},{64,7... | collective-permute-start | bytes 786440 | tf_op jit(solution)/shard_map/ppermute | solution.py:214
  43.8 1.9 %fusion.1 = bf16[32,8,5,64]{3,1,2,0:T(8,128)(2,1)S(1)} fusion(bf16[32,1,7,2,128]{4,2,3,0,1:T(8,128)(2,1)S(1)} %slice.148, bf16[32,1,8,5,128]{4,2,3,0,1:T(8,128)(2,1)S(1)} %copy.57, pred[8,5]{0,1:T(8,128)(4,1)S(1)} %copy-done.29, bf16[3,3,3,64,128]{4,3,2,1,0:T(8,128)(2,1)} %param.5), kind=kOutput, calls=%fused_computation.4 | convolution fusion | flops 186351616 | bytes 753704 | tf_op jit(solution)/shard_map/conv_general_dilated | solution.py:228
  46.1 0.6 copy-done.14
  53.3 42.3 %reduce_weight_grad.1 = f32[28,64,128]{2,1,0:T(8,128)S(1)} custom-call(f32[28,64,128]{2,1,0:T(8,128)S(1)} %constant_dynamic-update-slice_fusion.3.part_ref), custom_call_target="tpu_custom_call" | custom-call | tf_op jit(solution)/shard_map/reduce_weight_grad/pallas_call | solution.py:181
  95.5 1.0 slice.138
  96.6 0.5 slice_bitcast_fusion.3
  97.6 0.9 fusion
  99.0 0.9 fusion.2
  100.2 0.9 convert_element_type.73
  (126 shorter events, 8.5 us)
Async XLA Ops:
  0.6 12.0 %collective-permute-start = (bf16[1,1,32,2048]{3,2,1,0:T(8,128)(2,1)}, bf16[1,1,32,2048]{3,2,1,0:T(8,128)(2,1)S(1)}, u32[]{:S(2)}, u32[]{:S(2)}) collective-permute-start(bf16[1,1,32,2048]{3,2,1,0:T(8,128)(2,1)} %param.4), channel_id=1, source_target_pairs={{0,8},{8,16},{16,24},{24,32},{32,40},{40,48},{48,56},{56,64},{64,7... | collective-permute-start | bytes 393224 | tf_op jit(solution)/shard_map/ppermute | solution.py:214
  6.0 7.6 %collective-permute-start.1 = (bf16[1,1,32,2048]{3,2,1,0:T(8,128)(2,1)}, bf16[1,1,32,2048]{3,2,1,0:T(8,128)(2,1)S(1)}, u32[]{:S(2)}, u32[]{:S(2)}) collective-permute-start(bf16[1,1,32,2048]{3,2,1,0:T(8,128)(2,1)} %param.4), channel_id=1, source_target_pairs={{8,0},{16,8},{24,16},{32,24},{40,32},{48,40},{56,48},{64,56},{72,6... | collective-permute-start | bytes 393224 | tf_op jit(solution)/shard_map/ppermute | solution.py:215
  17.5 2.6 %copy-start.27 = (bf16[3,3,3,64,128]{4,3,2,1,0:T(8,128)(2,1)S(1)}, bf16[3,3,3,64,128]{4,3,2,1,0:T(8,128)(2,1)}, u32[]{:S(2)}) copy-start(bf16[3,3,3,64,128]{4,3,2,1,0:T(8,128)(2,1)} %param.5) | copy-start | bytes 1327108
  20.1 4.7 %copy-start.26 = (f32[128]{0:T(128)S(1)}, f32[128]{0:T(128)}, u32[]{:S(2)}) copy-start(f32[128]{0:T(128)} %param.6) | copy-start | bytes 1540
  20.1 9.4 %copy-start.22 = (bf16[1,1,32,2048]{3,2,1,0:T(8,128)(2,1)S(1)}, bf16[1,1,32,2048]{3,2,1,0:T(8,128)(2,1)}, u32[]{:S(2)}) copy-start(bf16[1,1,32,2048]{3,2,1,0:T(8,128)(2,1)} %copy-done.21) | copy-start | bytes 393220
  20.1 9.6 %copy-start.24 = (bf16[1,1,32,2048]{3,2,1,0:T(8,128)(2,1)S(1)}, bf16[1,1,32,2048]{3,2,1,0:T(8,128)(2,1)}, u32[]{:S(2)}) copy-start(bf16[1,1,32,2048]{3,2,1,0:T(8,128)(2,1)} %copy-done.23) | copy-start | bytes 393220
  24.8 5.2 %copy-start.25 = (bf16[1,8,16,128]{3,2,1,0:T(8,128)(2,1)S(1)}, bf16[1,8,16,128]{3,2,1,0:T(8,128)(2,1)}, u32[]{:S(2)}) copy-start(bf16[1,8,16,128]{3,2,1,0:T(8,128)(2,1)} %param.7) | copy-start | bytes 98308
  25.1 4.9 %collective-permute-start.3 = (f32[8,16,128]{2,1,0:T(8,128)S(1)}, f32[8,16,128]{2,1,0:T(8,128)S(1)}, u32[]{:S(2)}, u32[]{:S(2)}) collective-permute-start(f32[8,16,128]{2,1,0:T(8,128)S(1)} %constant_dynamic-slice_fusion), channel_id=1, source_target_pairs={{0,8},{8,0},{16,24},{24,16},{32,40},{40,32},{48,56},{56,48},{64,72... | collective-permute-start | bytes 196616 | tf_op jit(solution)/shard_map/ppermute | solution.py:223
  27.0 4.9 %collective-permute-start.2 = (f32[8,16,128]{2,1,0:T(8,128)S(1)}, f32[8,16,128]{2,1,0:T(8,128)S(1)}, u32[]{:S(2)}, u32[]{:S(2)}) collective-permute-start(f32[8,16,128]{2,1,0:T(8,128)S(1)} %constant_dynamic-slice_fusion.1), channel_id=1, source_target_pairs={{0,8},{8,0},{16,24},{24,16},{32,40},{40,32},{48,56},{56,48},{64,72... | collective-permute-start | bytes 196616 | tf_op jit(solution)/shard_map/ppermute | solution.py:223
  30.0 5.0 %collective-permute-start.5 = (f32[8,16,128]{2,1,0:T(8,128)S(1)}, f32[8,16,128]{2,1,0:T(8,128)S(1)}, u32[]{:S(2)}, u32[]{:S(2)}) collective-permute-start(f32[8,16,128]{2,1,0:T(8,128)S(1)} %get-tuple-element.7), channel_id=1, source_target_pairs={{0,8},{8,0},{16,24},{24,16},{32,40},{40,32},{48,56},{56,48},{64,72... | collective-permute-start | bytes 196616 | tf_op jit(solution)/shard_map/ppermute | solution.py:223
  32.6 3.3 %collective-permute-start.4 = (f32[8,16,128]{2,1,0:T(8,128)S(1)}, f32[8,16,128]{2,1,0:T(8,128)S(1)}, u32[]{:S(2)}, u32[]{:S(2)}) collective-permute-start(f32[8,16,128]{2,1,0:T(8,128)S(1)} %get-tuple-element.9), channel_id=1, source_target_pairs={{0,8},{8,0},{16,24},{24,16},{32,40},{40,32},{48,56},{56,48},{64,72... | collective-permute-start | bytes 196616 | tf_op jit(solution)/shard_map/ppermute | solution.py:223
  36.7 7.1 %copy-start.29 = (pred[8,5]{0,1:T(8,128)(4,1)S(1)}, pred[8,5]{0,1:T(8,128)(4,1)}, u32[]{:S(2)}) copy-start(pred[8,5]{0,1:T(8,128)(4,1)} %constant.60) | copy-start | bytes 124
  37.7 59.4 %collective-permute-start.6 = (bf16[1,1,32,4096]{3,2,1,0:T(8,128)(2,1)}, bf16[1,1,32,4096]{3,2,1,0:T(8,128)(2,1)S(1)}, u32[]{:S(2)}, u32[]{:S(2)}) collective-permute-start(bf16[1,1,32,4096]{3,2,1,0:T(8,128)(2,1)} %reshape.77), channel_id=1, source_target_pairs={{8,0},{16,8},{24,16},{32,24},{40,32},{48,40},{56,48},{64,56},{72,6... | collective-permute-start | bytes 786440 | tf_op jit(solution)/shard_map/ppermute | solution.py:215
  40.0 58.6 %collective-permute-start.7 = (bf16[1,1,32,4096]{3,2,1,0:T(8,128)(2,1)}, bf16[1,1,32,4096]{3,2,1,0:T(8,128)(2,1)S(1)}, u32[]{:S(2)}, u32[]{:S(2)}) collective-permute-start(bf16[1,1,32,4096]{3,2,1,0:T(8,128)(2,1)} %reshape.77), channel_id=1, source_target_pairs={{0,8},{8,16},{16,24},{24,32},{32,40},{40,48},{48,56},{56,64},{64,7... | collective-permute-start | bytes 786440 | tf_op jit(solution)/shard_map/ppermute | solution.py:214
  43.8 2.0 %copy-start.20 = (bf16[1,32,32,64]{3,2,1,0:T(8,128)(2,1)S(1)}, bf16[1,32,32,64]{3,2,1,0:T(8,128)(2,1)}, u32[]{:S(2)}) copy-start(bf16[1,32,32,64]{3,2,1,0:T(8,128)(2,1)} %get-tuple-element.34) | copy-start | bytes 393220
  45.8 1.9 %copy-start.11 = (bf16[1,32,32,64]{3,2,1,0:T(8,128)(2,1)S(1)}, bf16[1,32,32,64]{3,2,1,0:T(8,128)(2,1)}, u32[]{:S(2)}) copy-start(bf16[1,32,32,64]{3,2,1,0:T(8,128)(2,1)} %get-tuple-element.15) | copy-start | bytes 393220
  45.8 2.1 %copy-start.10 = (bf16[1,32,32,64]{3,2,1,0:T(8,128)(2,1)S(1)}, bf16[1,32,32,64]{3,2,1,0:T(8,128)(2,1)}, u32[]{:S(2)}) copy-start(bf16[1,32,32,64]{3,2,1,0:T(8,128)(2,1)} %get-tuple-element.16) | copy-start | bytes 393220
  46.6 1.5 %copy-start.9 = (bf16[1,32,32,64]{3,2,1,0:T(8,128)(2,1)S(1)}, bf16[1,32,32,64]{3,2,1,0:T(8,128)(2,1)}, u32[]{:S(2)}) copy-start(bf16[1,32,32,64]{3,2,1,0:T(8,128)(2,1)} %get-tuple-element.17) | copy-start | bytes 393220
  46.9 1.6 %copy-start.8 = (bf16[1,32,32,64]{3,2,1,0:T(8,128)(2,1)S(1)}, bf16[1,32,32,64]{3,2,1,0:T(8,128)(2,1)}, u32[]{:S(2)}) copy-start(bf16[1,32,32,64]{3,2,1,0:T(8,128)(2,1)} %get-tuple-element.18) | copy-start | bytes 393220
  47.2 1.6 %copy-start.7 = (bf16[1,32,32,64]{3,2,1,0:T(8,128)(2,1)S(1)}, bf16[1,32,32,64]{3,2,1,0:T(8,128)(2,1)}, u32[]{:S(2)}) copy-start(bf16[1,32,32,64]{3,2,1,0:T(8,128)(2,1)} %get-tuple-element.19) | copy-start | bytes 393220
  47.4 1.6 %copy-start.6 = (bf16[1,32,32,64]{3,2,1,0:T(8,128)(2,1)S(1)}, bf16[1,32,32,64]{3,2,1,0:T(8,128)(2,1)}, u32[]{:S(2)}) copy-start(bf16[1,32,32,64]{3,2,1,0:T(8,128)(2,1)} %get-tuple-element.20) | copy-start | bytes 393220
  47.7 1.6 %copy-start.5 = (bf16[1,32,32,64]{3,2,1,0:T(8,128)(2,1)S(1)}, bf16[1,32,32,64]{3,2,1,0:T(8,128)(2,1)}, u32[]{:S(2)}) copy-start(bf16[1,32,32,64]{3,2,1,0:T(8,128)(2,1)} %get-tuple-element.21) | copy-start | bytes 393220
  47.9 1.6 %copy-start.4 = (bf16[1,32,32,64]{3,2,1,0:T(8,128)(2,1)S(1)}, bf16[1,32,32,64]{3,2,1,0:T(8,128)(2,1)}, u32[]{:S(2)}) copy-start(bf16[1,32,32,64]{3,2,1,0:T(8,128)(2,1)} %get-tuple-element.22) | copy-start | bytes 393220
  48.2 1.6 %copy-start.15 = (bf16[1024,64]{1,0:T(8,128)(2,1)S(1)}, bf16[1024,64]{1,0:T(8,128)(2,1)}, u32[]{:S(2)}) copy-start(bf16[1024,64]{1,0:T(8,128)(2,1)} %reshape_squeeze.94) | copy-start | bytes 393220
  48.5 1.5 %copy-start.3 = (bf16[1,32,32,64]{3,2,1,0:T(8,128)(2,1)S(1)}, bf16[1,32,32,64]{3,2,1,0:T(8,128)(2,1)}, u32[]{:S(2)}) copy-start(bf16[1,32,32,64]{3,2,1,0:T(8,128)(2,1)} %get-tuple-element.23) | copy-start | bytes 393220
  48.7 1.5 %copy-start.2 = (bf16[1,32,32,64]{3,2,1,0:T(8,128)(2,1)S(1)}, bf16[1,32,32,64]{3,2,1,0:T(8,128)(2,1)}, u32[]{:S(2)}) copy-start(bf16[1,32,32,64]{3,2,1,0:T(8,128)(2,1)} %get-tuple-element.24) | copy-start | bytes 393220
  49.0 1.5 %copy-start.1 = (bf16[1,32,32,64]{3,2,1,0:T(8,128)(2,1)S(1)}, bf16[1,32,32,64]{3,2,1,0:T(8,128)(2,1)}, u32[]{:S(2)}) copy-start(bf16[1,32,32,64]{3,2,1,0:T(8,128)(2,1)} %get-tuple-element.25) | copy-start | bytes 393220
  49.2 1.5 %copy-start = (bf16[1,32,32,64]{3,2,1,0:T(8,128)(2,1)S(1)}, bf16[1,32,32,64]{3,2,1,0:T(8,128)(2,1)}, u32[]{:S(2)}) copy-start(bf16[1,32,32,64]{3,2,1,0:T(8,128)(2,1)} %get-tuple-element.26) | copy-start | bytes 393220
  50.3 1.5 %copy-start.19 = (bf16[1,32,32,64]{3,2,1,0:T(8,128)(2,1)S(1)}, bf16[1,32,32,64]{3,2,1,0:T(8,128)(2,1)}, u32[]{:S(2)}) copy-start(bf16[1,32,32,64]{3,2,1,0:T(8,128)(2,1)} %get-tuple-element.31) | copy-start | bytes 393220
  50.8 1.5 %copy-start.18 = (bf16[1,32,32,64]{3,2,1,0:T(8,128)(2,1)S(1)}, bf16[1,32,32,64]{3,2,1,0:T(8,128)(2,1)}, u32[]{:S(2)}) copy-start(bf16[1,32,32,64]{3,2,1,0:T(8,128)(2,1)} %get-tuple-element.32) | copy-start | bytes 393220
  51.0 1.5 %copy-start.17 = (bf16[1,32,32,64]{3,2,1,0:T(8,128)(2,1)S(1)}, bf16[1,32,32,64]{3,2,1,0:T(8,128)(2,1)}, u32[]{:S(2)}) copy-start(bf16[1,32,32,64]{3,2,1,0:T(8,128)(2,1)} %get-tuple-element.33) | copy-start | bytes 393220
  51.3 1.5 %copy-start.16 = (bf16[1,32,32,64]{3,2,1,0:T(8,128)(2,1)S(1)}, bf16[1,32,32,64]{3,2,1,0:T(8,128)(2,1)}, u32[]{:S(2)}) copy-start(bf16[1,32,32,64]{3,2,1,0:T(8,128)(2,1)} %get-tuple-element.30) | copy-start | bytes 393220
  (6 other events, 6.3 us)

commit v2 on v1

v2 whole, which is shorter than its diff:
```python
import jax
import jax.numpy as jnp
from jax import lax
from jax.experimental import pallas as pl
from jax.experimental.pallas import tpu as pltpu
from jax.sharding import PartitionSpec as P

MESH = pl.DeviceIdType.MESH
BF16 = jnp.bfloat16
F32 = jnp.float32
taps = 27
pieces = 28
per_kind = 14
side = 32
pairs = 16
cells = 512
loss_scale = 256.0
ring_order = (4, 3, 5, 2, 6, 1, 7)
plane_order = sorted(
    [(dx, dr) for dx in range(4) for dr in range(8) if (dx, dr) != (0, 0)],
    key=lambda d: -(min(d[0], 4 - d[0]) + min(d[1], 8 - d[1])),
)


def place():
    space = lax.axis_index("space")
    sample = lax.axis_index("sample")
    core = lax.rem(space, 2)
    z_lo = lax.rem(lax.div(space, 2), 4)
    y = lax.div(space, 8)
    z = lax.div(sample, 4) * 4 + z_lo
    x = lax.rem(sample, 4)
    return x, y, z, core


def ident(x, y, z, core):
    return ((y * 4 + lax.rem(z, 4)) * 2 + core, lax.div(z, 4) * 4 + x)


class Reduce:
    def __init__(self):
        self.x, self.y, self.z, self.core = place()
        x, y, z = self.x, self.y, self.z
        self.kind_a = x < 2
        self.ring_at = jnp.where(self.kind_a, z, y)
        self.row_at = jnp.where(self.kind_a, y, z)
        spot = lax.rem(x, 2) * 8 + self.row_at
        self.owner = spot < per_kind
        self.kind = jnp.where(self.kind_a, 0, 1)
        self.piece = jnp.minimum(self.kind * per_kind + spot, pieces - 1)
        self.slot = x * 8 + self.row_at
        self.partner = ident(x, y, z, 1 - self.core)
        plane = lax.axis_index("space")
        far_plane = plane + 2 * self.core - 1
        self.far_exists = jnp.logical_and(far_plane >= 0, far_plane < lax.axis_size("space"))
        self.far = (jnp.clip(far_plane, 0, lax.axis_size("space") - 1), lax.axis_index("sample"))
        self.near_tap = 2 - 2 * self.core
        self.far_tap = 2 * self.core

    def plane_peer(self, dx, dr):
        row = lax.rem(self.row_at + dr, 8)
        y = jnp.where(self.kind_a, row, self.y)
        z = jnp.where(self.kind_a, self.z, row)
        return ident(lax.rem(self.x + dx, 4), y, z, self.core)

    def ring_peer(self, dr):
        at = lax.rem(self.ring_at + dr, 8)
        y = jnp.where(self.kind_a, self.y, at)
        z = jnp.where(self.kind_a, at, self.z)
        return ident(self.x, y, z, self.core)

    def owner_of(self, piece):
        kind, spot = divmod(piece, per_kind)
        x = 2 * kind + spot // 8
        row = spot % 8
        if kind == 0:
            return ident(x, row, self.z, self.core), self.x * 8 + self.y
        return ident(x, self.y, row, self.core), self.x * 8 + self.z


def signal(sem, who):
    pl.semaphore_signal(sem, inc=1, device_id=who, device_id_type=MESH)


def remote(src, dst, send, recv, who):
    return pltpu.make_async_remote_copy(
        src_ref=src, dst_ref=dst, send_sem=send, recv_sem=recv, device_id=who, device_id_type=MESH
    )


def local(src, dst, sem):
    return pltpu.make_async_copy(src, dst, sem)


def lay_weights(wraw, wf, wb):
    none = jnp.zeros((64, 128), BF16)
    for a in range(3):
        for b in range(3):
            t0, t1, t2 = (wraw[a, b, c] for c in range(3))
            for cell, column in enumerate(((t1, t2, none, t0), (t0, t1, t2, none))):
                for k, block in enumerate(column):
                    wf[a, 256 * b + 64 * k : 256 * b + 64 * k + 64, 128 * cell : 128 * cell + 128] = block
            for cell, row in enumerate(((t2, t1, t0, none), (none, t2, t1, t0))):
                at = (2 * a + cell) * 64
                for j, block in enumerate(row):
                    wb[b, at : at + 64, 128 * j : 128 * j + 128] = block


def lay_plane(xin, xk, p):
    width = 512
    row = lax.broadcasted_iota(jnp.int32, (side, width), 0)
    low = lax.rem(lax.broadcasted_iota(jnp.int32, (side, width), 1), 128) < 64
    first, last = row == 0, row == side - 1
    for chunk in range(4):
        at = width * chunk
        left = xin[p, :, at : at + width].astype(F32)
        here = xin[p, :, at + 128 : at + 128 + width].astype(F32)
        right = xin[p, :, at + 256 : at + 256 + width].astype(F32)
        beside = jnp.where(low, right, left)
        for k, value in enumerate((here, beside)):
            up = jnp.where(first, 0.0, pltpu.roll(value, 1, 0))
            down = jnp.where(last, 0.0, pltpu.roll(value, side - 1, 0))
            for b, shifted in enumerate((up, value, down)):
                shifted = shifted.astype(BF16)
                for i in range(4):
                    q = 4 * chunk + i
                    lane = 256 * b + 128 * k
                    xk[p, side * q : side * q + side, lane : lane + 128] = shifted[:, 128 * i : 128 * i + 128]


def flip_plane(xk, xt, p):
    xt[p] = xk[p, :, 256:512].T


def block_kernel(
    volume_ref, weight_ref, bias_ref, cot_ref,
    pooled_ref, input_grad_ref, total_ref,
    xin, wraw, cots, wf, wb, xk, xt, pre, act, pe, sum_e, sum_n, sums, psums, ctab, pvt, fa, fb, gs, part, bt, in_bt,
    mine, theirs, rows, rs, ring_src, ring, final, gath,
    load_sem, halo_send, halo_recv, cot_send, cot_recv, pool_send, pool_recv, bt_send, bt_recv,
    core_send, core_recv, rs_send, rs_recv, ring_send, ring_recv, ag_send, ag_recv, fw_send, fw_recv,
):
    r = Reduce()
    core = r.core
    near, far = r.near_tap, r.far_tap
    body_lanes = pl.ds(128, 2048)
    loads = [
        local(volume_ref.at[0, 0], xin.at[1, :, body_lanes], load_sem.at[0]),
        local(cot_ref.at[0], cots.at[core], load_sem.at[1]),
        local(weight_ref, wraw, load_sem.at[2]),
    ]
    for cp in loads:
        cp.start()
    bar = pltpu.get_barrier_semaphore()

    @pl.when(r.owner)
    def _():
        for dx, dr in plane_order:
            signal(bar, r.plane_peer(dx, dr))

    @pl.when(r.far_exists)
    def _():
        signal(bar, r.far)

    @pl.when(r.owner)
    def _():
        for dr in ring_order:
            signal(bar, r.ring_peer(dr))

    signal(bar, r.partner)
    for p in range(3):
        xin[p, :, 0:128] = jnp.zeros((side, 128), BF16)
        xin[p, :, 2176:2304] = jnp.zeros((side, 128), BF16)

    @pl.when(jnp.logical_not(r.far_exists))
    def _():
        xin[far] = jnp.zeros((side, 2304), BF16)
        in_bt[2 - far] = jnp.zeros((cells, 128), BF16)

    for cp in loads:
        cp.wait()
    own = jnp.where(r.owner, 1, 0)
    pl.semaphore_wait(bar, pieces + 1 + 6 * own + jnp.where(r.far_exists, 1, 0))

    own_plane = xin.at[1, :, body_lanes]
    far_halo = remote(own_plane, xin.at[2 - far, :, body_lanes], halo_send.at[0], halo_recv.at[0], r.far)

    @pl.when(r.far_exists)
    def _():
        far_halo.start()

    near_halo = remote(own_plane, xin.at[2 - near, :, body_lanes], halo_send.at[1], halo_recv.at[1], r.partner)
    near_halo.start()
    cot_copy = remote(cots.at[core], cots.at[core], cot_send, cot_recv, r.partner)
    cot_copy.start()

    lay_weights(wraw, wf, wb)
    for b in range(3):
        gs[b, 0:side, :] = jnp.zeros((side, 256), BF16)
        gs[b, side + cells : 2 * side + cells, :] = jnp.zeros((side, 256), BF16)
    lay_plane(xin, xk, 1)
    flip_plane(xk, xt, 1)
    near_halo.wait_recv()
    lay_plane(xin, xk, near)
    bias = bias_ref[...].reshape(1, 128)
    bias = jnp.concatenate([bias, bias], axis=1)
    for m in range(4):
        span = pl.ds(128 * m, 128)
        pre[span] = (
            bias
            + jnp.dot(xk[1, span], wf[1], preferred_element_type=F32)
            + jnp.dot(xk[near, span], wf[near], preferred_element_type=F32)
        )
    flip_plane(xk, xt, near)
    cot_copy.wait_recv()
    for half in range(2):
        for row in range(8):
            ctab[pl.ds(8 * half + row, 16, stride=16), :] = cots[half, row].astype(F32)

    @pl.when(r.far_exists)
    def _():
        far_halo.wait_recv()

    lay_plane(xin, xk, far)
    pool_copies = []
    for m in range(4):
        span = pl.ds(128 * m, 128)
        v = pre[span] + jnp.dot(xk[far, span], wf[far], preferred_element_type=F32)
        s = 0.5 * jnp.tanh(0.5 * v) + 0.5
        z = v * s
        e = jnp.exp(z)
        act[span] = z
        pe[span] = e * (s * (1.0 + (v - z)))
        n = e * z
        sum_e[span] = e[:, :128] + e[:, 128:]
        sum_n[span] = n[:, :128] + n[:, 128:]
        half = pl.ds(64 * m, 64)
        even = pl.ds(128 * m, 64, stride=2)
        odd = pl.ds(128 * m + 1, 64, stride=2)
        sums[m, 0] = sum_e[even, :] + sum_e[odd, :]
        sums[m, 1] = sum_n[even, :] + sum_n[odd, :]
        cp = remote(sums.at[m], psums.at[m], pool_send.at[m], pool_recv.at[m], r.partner)
        cp.start()
        pool_copies.append(cp)
    flip_plane(xk, xt, far)
    row = lax.rem(lax.broadcasted_iota(jnp.int32, (128, 256), 0), side)
    bias_part = jnp.zeros((1, 256), F32)
    for m in range(4):
        pool_copies[m].wait_recv()
        den = sums[m, 0] + psums[m, 0]
        value = (sums[m, 1] + psums[m, 1]) / den
        half = pl.ds(64 * m, 64)
        pvt[half] = value
        cb = ctab[half] / den
        ca = cb * (1.0 - value)
        even = pl.ds(128 * m, 64, stride=2)
        odd = pl.ds(128 * m + 1, 64, stride=2)
        fa[even, :] = ca
        fa[odd, :] = ca
        fb[even, :] = cb
        fb[odd, :] = cb
        span = pl.ds(128 * m, 128)
        wide_a = jnp.concatenate([fa[span], fa[span]], axis=1)
        wide_b = jnp.concatenate([fb[span], fb[span]], axis=1)
        g = (pe[span] * (wide_a + wide_b * act[span])).astype(BF16)
        gs[1, side + 128 * m : side + 128 * m + 128, :] = g
        g = g.astype(F32)
        bias_part = bias_part + jnp.sum(g, axis=0, keepdims=True)
        after = jnp.where(row == side - 1, 0.0, pltpu.roll(g, 127, 0))
        before = jnp.where(row == 0, 0.0, pltpu.roll(g, 1, 0))
        gs[0, side + 128 * m : side + 128 * m + 128, :] = after.astype(BF16)
        gs[2, side + 128 * m : side + 128 * m + 128, :] = before.astype(BF16)

    half = pl.ds(pl.multiple_of(core * 32, 32), 32)
    far_half = pl.ds(pl.multiple_of(32 - core * 32, 32), 32)
    core_copies = []
    part[27] = jnp.zeros((64, 128), F32)
    part[27, 0:1, :] = bias_part[:, :128] + bias_part[:, 128:]
    for a in range(3):
        for b in range(3):
            g = a * 3 + b
            block = jnp.dot(xt[a], gs[b, side : side + cells, :], preferred_element_type=F32)
            part[3 * g] = block[192:256, :128] + block[0:64, 128:]
            part[3 * g + 1] = block[0:64, :128] + block[64:128, 128:]
            part[3 * g + 2] = block[64:128, :128] + block[128:192, 128:]
            span = pl.ds(3 * g, 3 if g < 8 else 4)
            mine[span] = part[span, far_half, :].astype(BF16)
            cp = remote(mine.at[span], theirs.at[span], core_send.at[g], core_recv.at[g], r.partner)
            cp.start()
            core_copies.append(cp)
    rs_copies = []
    for g in range(9):
        count = 3 if g < 8 else 4
        span = pl.ds(3 * g, count)
        core_copies[g].wait_recv()
        rows[span] = (part[span, half, :] + theirs[span].astype(F32)).astype(BF16)
        for piece in range(3 * g, 3 * g + count):
            who, slot = r.owner_of(piece)
            is_me = jnp.logical_and(r.owner, r.piece == piece)
            cp = remote(rows.at[piece], rs.at[slot], rs_send.at[piece], rs_recv, who)
            rs_copies.append((is_me, cp))

            @pl.when(jnp.logical_not(is_me))
            def _(cp=cp):
                cp.start()

            @pl.when(is_me)
            def _(piece=piece):
                local(rows.at[piece], rs.at[r.slot], rs_recv).start()

    for m in range(4):
        at = 128 * m
        total = jnp.zeros((128, 384), F32)
        for b in range(3):
            wide = jnp.concatenate(
                [
                    gs[b, at : at + 128, 128:256],
                    gs[b, at + 32 : at + 160, :],
                    gs[b, at + 64 : at + 192, 0:128],
                ],
                axis=1,
            )
            total = total + lax.dot_general(
                wide, wb[b], (((1,), (1,)), ((), ())), preferred_element_type=F32
            )
        for a in range(3):
            bt[a, at : at + 128, :] = total[:, 128 * a : 128 * a + 128].astype(BF16)
    bt_far = remote(bt.at[far], in_bt.at[far], bt_send.at[0], bt_recv.at[0], r.far)

    @pl.when(r.far_exists)
    def _():
        bt_far.start()

    bt_near = remote(bt.at[near], in_bt.at[near], bt_send.at[1], bt_recv.at[1], r.partner)
    bt_near.start()
    for row in range(8):
        pooled_ref[0, row] = pvt[pl.ds(8 * core + row, 16, stride=16), :].astype(BF16)

    @pl.when(r.owner)
    def _():
        local(rs, rs, rs_recv).wait()
        total = rs[0].astype(F32)
        for i in range(1, 32):
            total = total + rs[i].astype(F32)
        ring_src[...] = total.astype(BF16)
        copies = []
        for dr in ring_order:
            cp = remote(ring_src, ring.at[r.ring_at], ring_send.at[dr], ring_recv, r.ring_peer(dr))
            cp.start()
            copies.append(cp)
        local(ring_src, ring.at[r.ring_at], ring_recv).start()
        local(ring, ring, ring_recv).wait()
        total = ring[0].astype(F32)
        for i in range(1, 8):
            total = total + ring[i].astype(F32)
        final[...] = total.astype(BF16)
        for i, (dx, dr) in enumerate(plane_order):
            cp = remote(final, gath.at[core, r.piece], ag_send.at[i], ag_recv.at[r.kind], r.plane_peer(dx, dr))
            cp.start()
            copies.append(cp)
        local(final, gath.at[core, r.piece], ag_recv.at[r.kind]).start()
        for cp in copies:
            cp.wait_send()

    bt_near.wait()

    @pl.when(r.far_exists)
    def _():
        bt_far.wait()

    for q in range(pairs):
        span = pl.ds(side * q, side)
        summed = in_bt[0, span].astype(F32) + bt[1, span].astype(F32) + in_bt[2, span].astype(F32)
        input_grad_ref[0, 0, :, 128 * q : 128 * q + 128] = summed.astype(BF16)

    fw_copies = []
    for kind in range(2):
        span = gath.at[core, pl.ds(per_kind * kind, per_kind)]
        local(span, span, ag_recv.at[kind]).wait()
        cp = remote(span, span, fw_send.at[kind], fw_recv.at[kind], r.partner)
        cp.start()
        fw_copies.append(cp)
    for cp in core_copies + pool_copies + [near_halo, cot_copy]:
        cp.wait_send()

    @pl.when(r.far_exists)
    def _():
        far_halo.wait_send()

    for is_me, cp in rs_copies:

        @pl.when(jnp.logical_not(is_me))
        def _(cp=cp):
            cp.wait_send()

    for cp in fw_copies:
        cp.wait()
    for h in range(2):
        total_ref[:, 32 * h : 32 * h + 32, :] = gath[h].astype(F32) * (1.0 / loss_scale)


def block(volume, weight, conv_bias, cotangent):
    dma = pltpu.SemaphoreType.DMA
    vmem = pltpu.VMEM
    anywhere = pl.BlockSpec(memory_space=pl.ANY)
    here = pl.BlockSpec(memory_space=pltpu.VMEM)
    pooled, input_grad, total = pl.pallas_call(
        block_kernel,
        out_shape=(
            jax.ShapeDtypeStruct(cotangent.shape, BF16),
            jax.ShapeDtypeStruct(volume.shape, BF16),
            jax.ShapeDtypeStruct((pieces, 64, 128), F32),
        ),
        in_specs=[anywhere, anywhere, here, anywhere],
        out_specs=(here, here, here),
        scratch_shapes=[
            vmem((3, side, 2304), BF16),
            vmem((3, 3, 3, 64, 128), BF16),
            vmem((2, 8, 16, 128), BF16),
            vmem((3, 768, 256), BF16),
            vmem((3, 384, 512), BF16),
            vmem((3, cells, 768), BF16),
            vmem((3, 256, cells), BF16),
            vmem((cells, 256), F32),
            vmem((cells, 256), F32),
            vmem((cells, 256), F32),
            vmem((cells, 128), F32),
            vmem((cells, 128), F32),
            vmem((4, 2, 64, 128), F32),
            vmem((4, 2, 64, 128), F32),
            vmem((256, 128), F32),
            vmem((256, 128), F32),
            vmem((cells, 128), F32),
            vmem((cells, 128), F32),
            vmem((3, cells + 2 * side, 256), BF16),
            vmem((pieces, 64, 128), F32),
            vmem((3, cells, 128), BF16),
            vmem((3, cells, 128), BF16),
            vmem((pieces, 32, 128), BF16),
            vmem((pieces, 32, 128), BF16),
            vmem((pieces, 32, 128), BF16),
            vmem((32, 32, 128), BF16),
            vmem((32, 128), BF16),
            vmem((8, 32, 128), BF16),
            vmem((32, 128), BF16),
            vmem((2, pieces, 32, 128), BF16),
            dma((3,)), dma((2,)), dma((2,)), dma, dma, dma((4,)), dma((4,)), dma((2,)), dma((2,)),
            dma((9,)), dma((9,)), dma((pieces,)), dma, dma((8,)), dma, dma((31,)), dma((2,)), dma((2,)), dma((2,)),
        ],
        compiler_params=pltpu.CompilerParams(
            collective_id=0, has_side_effects=True, vmem_limit_bytes=48 * 2**20
        ),
        name="conv_block",
    )(volume, weight, conv_bias, cotangent)
    return pooled, input_grad, total[:taps].reshape(weight.shape), total[taps, 0]


def solution(mesh):
    placed = (P("sample", "space", None, None), P(), P(), P("sample", "space", None, None))
    return jax.shard_map(
        block,
        mesh=mesh,
        in_specs=placed,
        out_specs=(P("sample", "space", None, None), P("sample", "space", None, None), P(), P()),
        check_vma=False,
    )
```

time: 102 us -> 56.3 us (0.55)
  starting transfers between devices: 24.5 us -> 0 us
  matrix products: 14.7 us -> 0 us
  local copies, waits for them, and re-layouts: 15.6 us -> 6.07 us
  Pallas kernels: 42.3 us -> 49.3 us
  other arithmetic: 1.5 us -> 0 us
  between operations: 1.69 us -> 0.65 us
    ppermute x8 -> x0, starting transfers between devices: 24.5 us -> none  [the longest x2 8.87 us: extended(): before = lax.ppermute(last, axis, up)]
    conv_general_dilated x4 -> x0, matrix products: 8.38 us -> none  [the longest x1 4.68 us: local(): lax.conv_general_dilated(near_cells, weight, (1, 1, 1), ((0, 0), (1, 1),...]
    pallas_call x1, Pallas kernels: 42.3 us -> 49.3 us  [block(): pl.pallas_call(block_kernel, out_shape=(jax.ShapeDtypeStruct(cotangent.sh...]
    dot_general x27 -> x0, matrix products: 6.33 us -> none  [local(): lax.dot_general(window, flat_grad, (((0,), (0,)), ((), ())), preferred_el...]
    slice x6 -> x1, local copies, waits for them, and re-layouts: 4.94 us -> 0.97 us  [block(): total[:taps].reshape(weight.shape)]
    another operation x4 -> x0, local copies, waits for them, and re-layouts: 3.17 us -> none  [the longest x3 2.37 us: local(): window = padded[depth_tap, row_tap:row_tap + side_cells, col_tap:col_tap...]
    reshape x2 -> x0, local copies, waits for them, and re-layouts: 1.91 us -> none  [the longest x1 1.1 us: local(): near_cells = planes.reshape(1, 3, side_cells, side_cells, chan_in)]
    unnamed x67 -> x10, local copies, waits for them, and re-layouts: 2.8 us -> 4.59 us
  transfers between devices with their start and end apart: 8 -> 0, of which waited for: 1 -> 0; matrix products, arithmetic and copies ran while one was open for 15% -> 0% of each run, Pallas kernels for 42% -> 0%
where the time goes in v2:
time: 56.3 us; the launch traced here: 56 us
  Pallas kernels  49.3 us (88%)
  local copies, waits for them, and re-layouts  6.07 us (11%)
  between operations  0.65 us (1%)
    pallas_call x1, Pallas kernels, block(): pl.pallas_call(block_kernel, out_shape=(jax.ShapeDtypeStruct(cotangent.sh...  49.3 us
    unnamed x10, local copies, waits for them, and re-layouts  4.59 us

profile of v2, /device:TPU:1, one launch (start us, length us, event | category | flops | bytes accessed | tf_op | source)
XLA Modules:
  0.0 56.0 jit_solution(15744745650639216635)
XLA Ops:
  0.6 0.0 copy-start
  0.6 1.0 %copy-done = bf16[3,3,3,64,128]{4,3,2,1,0:T(8,128)(2,1)S(1)} copy-done((bf16[3,3,3,64,128]{4,3,2,1,0:T(8,128)(2,1)S(1)}, bf16[3,3,3,64,128]{4,3,2,1,0:T(8,128)(2,1)}, u32[]{:S(2)}) %copy-start) | copy-done | bytes 442392
  1.6 0.0 copy-start.1
  1.6 0.9 %copy-done.1 = bf16[1,1,32,2048]{3,2,1,0:T(8,128)(2,1)S(1)} copy-done((bf16[1,1,32,2048]{3,2,1,0:T(8,128)(2,1)S(1)}, bf16[1,1,32,2048]{3,2,1,0:T(8,128)(2,1)}, u32[]{:S(2)}) %copy-start.1) | copy-done | bytes 131096
  2.6 0.0 copy-start.2
  2.6 0.8 %copy-done.2 = bf16[1,8,16,128]{3,2,1,0:T(8,128)(2,1)S(1)} copy-done((bf16[1,8,16,128]{3,2,1,0:T(8,128)(2,1)S(1)}, bf16[1,8,16,128]{3,2,1,0:T(8,128)(2,1)}, u32[]{:S(2)}) %copy-start.2) | copy-done | bytes 32792
  3.3 0.0 copy-start.3
  3.3 0.7 %copy-done.3 = f32[128]{0:T(128)S(1)} copy-done((f32[128]{0:T(128)S(1)}, f32[128]{0:T(128)}, u32[]{:S(2)}) %copy-start.3) | copy-done | bytes 536
  4.0 49.3 %conv_block.1 = (bf16[1,8,16,128]{3,2,1,0:T(8,128)(2,1)S(1)}, bf16[1,1,32,2048]{3,2,1,0:T(8,128)(2,1)S(1)}, f32[28,64,128]{2,1,0:T(8,128)S(1)}) custom-call(bf16[1,1,32,2048]{3,2,1,0:T(8,128)(2,1)S(1)} %copy-done.1, bf16[3,3,3,64,128]{4,3,2,1,0:T(8,128)(2,1)S(1)} %copy-done, f32[128]{0:T(128)S(1)} %copy-done.3, bf16[1,8,16,128]{3,2,1,0:T(8,128)(2,1)S(1)} %copy-done.2), custom_call_target="tpu_custom_call" | custom-call | tf_op jit(solution)/shard_map/conv_block/pallas_call | solution.py:407
  53.2 0.5 slice_bitcast_fusion
  53.8 1.0 %slice.6 = f32[27,64,128]{2,1,0:T(8,128)} slice(f32[28,64,128]{2,1,0:T(8,128)S(1)} %get-tuple-element.9), slice={[0:27], [0:64], [0:128]} | slice | bytes 1769472 | tf_op jit(solution)/shard_map/slice | solution.py:455
  54.7 0.6 %copy.10 = bf16[1,8,16,128]{3,2,1,0:T(8,128)(2,1)} copy(bf16[1,8,16,128]{3,2,1,0:T(8,128)(2,1)S(1)} %get-tuple-element.14) | data formatting | bytes 65536
  55.3 0.7 %copy.11 = bf16[1,1,32,2048]{3,2,1,0:T(8,128)(2,1)} copy(bf16[1,1,32,2048]{3,2,1,0:T(8,128)(2,1)S(1)} %get-tuple-element.15) | data formatting | bytes 262144
Async XLA Ops:
  0.6 1.0 %copy-start = (bf16[3,3,3,64,128]{4,3,2,1,0:T(8,128)(2,1)S(1)}, bf16[3,3,3,64,128]{4,3,2,1,0:T(8,128)(2,1)}, u32[]{:S(2)}) copy-start(bf16[3,3,3,64,128]{4,3,2,1,0:T(8,128)(2,1)} %weight_ref.1) | copy-start | bytes 1327108
  1.6 0.9 %copy-start.1 = (bf16[1,1,32,2048]{3,2,1,0:T(8,128)(2,1)S(1)}, bf16[1,1,32,2048]{3,2,1,0:T(8,128)(2,1)}, u32[]{:S(2)}) copy-start(bf16[1,1,32,2048]{3,2,1,0:T(8,128)(2,1)} %volume_ref.1) | copy-start | bytes 393220
  2.6 0.8 %copy-start.2 = (bf16[1,8,16,128]{3,2,1,0:T(8,128)(2,1)S(1)}, bf16[1,8,16,128]{3,2,1,0:T(8,128)(2,1)}, u32[]{:S(2)}) copy-start(bf16[1,8,16,128]{3,2,1,0:T(8,128)(2,1)} %cot_ref.1) | copy-start | bytes 98308
  3.3 0.7 %copy-start.3 = (f32[128]{0:T(128)S(1)}, f32[128]{0:T(128)}, u32[]{:S(2)}) copy-start(f32[128]{0:T(128)} %bias_ref.1) | copy-start | bytes 1540

commit v3 on v2

--- a/solution.py
+++ b/solution.py
@@ -9,17 +9,16 @@
 BF16 = jnp.bfloat16
 F32 = jnp.float32
 taps = 27
-pieces = 28
-per_kind = 14
+blocks = 28
+per_piece = 1
+pieces = blocks // per_piece
+per_kind = pieces // 2
 side = 32
 pairs = 16
 cells = 512
 loss_scale = 256.0
-ring_order = (4, 3, 5, 2, 6, 1, 7)
-plane_order = sorted(
-    [(dx, dr) for dx in range(4) for dr in range(8) if (dx, dr) != (0, 0)],
-    key=lambda d: -(min(d[0], 4 - d[0]) + min(d[1], 8 - d[1])),
-)
+plane_order = sorted(((x, row) for x in range(4) for row in range(8)), key=sum)
+spots = tuple((x, row) for row in range(7) for x in range(2))
 
 
 def place():
@@ -44,10 +43,15 @@
         self.kind_a = x < 2
         self.ring_at = jnp.where(self.kind_a, z, y)
         self.row_at = jnp.where(self.kind_a, y, z)
-        spot = lax.rem(x, 2) * 8 + self.row_at
-        self.owner = spot < per_kind
         self.kind = jnp.where(self.kind_a, 0, 1)
-        self.piece = jnp.minimum(self.kind * per_kind + spot, pieces - 1)
+        side_x = jnp.where(self.kind_a, x, 3 - x)
+        self.owner = False
+        self.piece = 0
+        for i, (sx, row) in enumerate(spots):
+            here = jnp.logical_and(side_x == sx, self.row_at == row)
+            self.owner = jnp.logical_or(self.owner, here)
+            self.piece = self.piece + jnp.where(here, i, 0)
+        self.piece = self.piece + self.kind * per_kind
         self.slot = x * 8 + self.row_at
         self.partner = ident(x, y, z, 1 - self.core)
         plane = lax.axis_index("space")
@@ -57,25 +61,28 @@
         self.near_tap = 2 - 2 * self.core
         self.far_tap = 2 * self.core
 
-    def plane_peer(self, dx, dr):
-        row = lax.rem(self.row_at + dr, 8)
+    def plane_peer(self, x, row):
         y = jnp.where(self.kind_a, row, self.y)
         z = jnp.where(self.kind_a, self.z, row)
-        return ident(lax.rem(self.x + dx, 4), y, z, self.core)
-
-    def ring_peer(self, dr):
-        at = lax.rem(self.ring_at + dr, 8)
+        return ident(x, y, z, self.core), jnp.logical_and(self.x == x, self.row_at == row)
+
+    def ring_peer(self, at):
         y = jnp.where(self.kind_a, self.y, at)
         z = jnp.where(self.kind_a, at, self.z)
-        return ident(self.x, y, z, self.core)
+        return ident(self.x, y, z, self.core), self.ring_at == at
 
     def owner_of(self, piece):
-        kind, spot = divmod(piece, per_kind)
-        x = 2 * kind + spot // 8
-        row = spot % 8
+        kind, i = divmod(piece, per_kind)
+        x, row = spots[i]
         if kind == 0:
             return ident(x, row, self.z, self.core), self.x * 8 + self.y
-        return ident(x, self.y, row, self.core), self.x * 8 + self.z
+        return ident(3 - x, self.y, row, self.core), self.x * 8 + self.z
+
+
+def unless(me, action, otherwise=None):
+    pl.when(jnp.logical_not(me))(action)
+    if otherwise is not None:
+        pl.when(me)(otherwise)
 
 
 def signal(sem, who):
@@ -133,41 +140,43 @@
 
 
 def block_kernel(
-    volume_ref, weight_ref, bias_ref, cot_ref,
-    pooled_ref, input_grad_ref, total_ref,
-    xin, wraw, cots, wf, wb, xk, xt, pre, act, pe, sum_e, sum_n, sums, psums, ctab, pvt, fa, fb, gs, part, bt, in_bt,
-    mine, theirs, rows, rs, ring_src, ring, final, gath,
+    volume_ref, weight_ref, bias_hbm, cot_ref,
+    pooled_ref, input_grad_ref, weight_grad_ref, bias_grad_ref,
+    xin, wraw, bias_ref, cots, wf, wb, xk, xt, pre, act, pe, sum_e, sum_n, sums, psums, ctab, pvt, fa, fb, gs, part, bt, in_bt,
+    mine, theirs, rows, rs, ring_src, ring, final,
+    gath, pooled_out, input_grad_out, weights, bias_out,
     load_sem, halo_send, halo_recv, cot_send, cot_recv, pool_send, pool_recv, bt_send, bt_recv,
-    core_send, core_recv, rs_send, rs_recv, ring_send, ring_recv, ag_send, ag_recv, fw_send, fw_recv,
+    core_send, core_recv, rs_send, rs_recv, ring_send, ring_recv, ag_send, ag_recv, fw_send, fw_recv, out_sem,
 ):
     r = Reduce()
     core = r.core
     near, far = r.near_tap, r.far_tap
     body_lanes = pl.ds(128, 2048)
+    bar = pltpu.get_barrier_semaphore()
+
+    @pl.when(r.far_exists)
+    def _():
+        signal(bar, r.far)
+
+    signal(bar, r.partner)
     loads = [
         local(volume_ref.at[0, 0], xin.at[1, :, body_lanes], load_sem.at[0]),
         local(cot_ref.at[0], cots.at[core], load_sem.at[1]),
         local(weight_ref, wraw, load_sem.at[2]),
+        local(bias_hbm, bias_ref, load_sem.at[3]),
     ]
     for cp in loads:
         cp.start()
-    bar = pltpu.get_barrier_semaphore()
 
     @pl.when(r.owner)
     def _():
-        for dx, dr in plane_order:
-            signal(bar, r.plane_peer(dx, dr))
-
-    @pl.when(r.far_exists)
-    def _():
-        signal(bar, r.far)
-
-    @pl.when(r.owner)
-    def _():
-        for dr in ring_order:
-            signal(bar, r.ring_peer(dr))
-
-    signal(bar, r.partner)
+        for x, row in reversed(plane_order):
+            who, me = r.plane_peer(x, row)
+            unless(me, lambda who=who: signal(bar, who))
+        for at in range(8):
+            who, me = r.ring_peer(at)
+            unless(me, lambda who=who: signal(bar, who))
+
     for p in range(3):
         xin[p, :, 0:128] = jnp.zeros((side, 128), BF16)
         xin[p, :, 2176:2304] = jnp.zeros((side, 128), BF16)
@@ -289,24 +298,21 @@
             cp.start()
             core_copies.append(cp)
     rs_copies = []
+    sent = 0
     for g in range(9):
         count = 3 if g < 8 else 4
         span = pl.ds(3 * g, count)
         core_copies[g].wait_recv()
         rows[span] = (part[span, half, :] + theirs[span].astype(F32)).astype(BF16)
-        for piece in range(3 * g, 3 * g + count):
-            who, slot = r.owner_of(piece)
-            is_me = jnp.logical_and(r.owner, r.piece == piece)
-            cp = remote(rows.at[piece], rs.at[slot], rs_send.at[piece], rs_recv, who)
+        while sent < pieces and per_piece * (sent + 1) <= 3 * g + count:
+            who, slot = r.owner_of(sent)
+            is_me = jnp.logical_and(r.owner, r.piece == sent)
+            taps_of = rows.at[pl.ds(per_piece * sent, per_piece)]
+            cp = remote(taps_of, rs.at[slot], rs_send.at[sent], rs_recv, who)
+            keep = local(taps_of, rs.at[r.slot], rs_recv)
+            unless(is_me, cp.start, keep.start)
             rs_copies.append((is_me, cp))
-
-            @pl.when(jnp.logical_not(is_me))
-            def _(cp=cp):
-                cp.start()
-
-            @pl.when(is_me)
-            def _(piece=piece):
-                local(rows.at[piece], rs.at[r.slot], rs_recv).start()
+            sent += 1
 
     for m in range(4):
         at = 128 * m
@@ -334,8 +340,10 @@
     bt_near = remote(bt.at[near], in_bt.at[near], bt_send.at[1], bt_recv.at[1], r.partner)
     bt_near.start()
     for row in range(8):
-        pooled_ref[0, row] = pvt[pl.ds(8 * core + row, 16, stride=16), :].astype(BF16)
-
+        pooled_out[row] = pvt[pl.ds(8 * core + row, 16, stride=16), :].astype(BF16)
+
+    outs = [local(pooled_out, pooled_ref.at[0], out_sem.at[0])]
+    outs[0].start()
     @pl.when(r.owner)
     def _():
         local(rs, rs, rs_recv).wait()
@@ -343,24 +351,25 @@
         for i in range(1, 32):
             total = total + rs[i].astype(F32)
         ring_src[...] = total.astype(BF16)
-        copies = []
-        for dr in ring_order:
-            cp = remote(ring_src, ring.at[r.ring_at], ring_send.at[dr], ring_recv, r.ring_peer(dr))
-            cp.start()
-            copies.append(cp)
-        local(ring_src, ring.at[r.ring_at], ring_recv).start()
+        ring_copies = []
+        for at in range(8):
+            who, me = r.ring_peer(at)
+            cp = remote(ring_src, ring.at[r.ring_at], ring_send.at[at], ring_recv, who)
+            unless(me, cp.start, local(ring_src, ring.at[r.ring_at], ring_recv).start)
+            ring_copies.append((me, cp))
         local(ring, ring, ring_recv).wait()
         total = ring[0].astype(F32)
         for i in range(1, 8):
             total = total + ring[i].astype(F32)
         final[...] = total.astype(BF16)
-        for i, (dx, dr) in enumerate(plane_order):
-            cp = remote(final, gath.at[core, r.piece], ag_send.at[i], ag_recv.at[r.kind], r.plane_peer(dx, dr))
-            cp.start()
-            copies.append(cp)
-        local(final, gath.at[core, r.piece], ag_recv.at[r.kind]).start()
-        for cp in copies:
-            cp.wait_send()
+        place_of = gath.at[core, pl.ds(per_piece * r.piece, per_piece)]
+        for i, (x, row) in enumerate(plane_order):
+            who, me = r.plane_peer(x, row)
+            cp = remote(final, place_of, ag_send.at[i], ag_recv.at[r.kind], who)
+            unless(me, cp.start, local(final, place_of, ag_recv.at[r.kind]).start)
+            ring_copies.append((me, cp))
+        for me, cp in ring_copies:
+            unless(me, cp.wait_send)
 
     bt_near.wait()
 
@@ -371,11 +380,13 @@
     for q in range(pairs):
         span = pl.ds(side * q, side)
         summed = in_bt[0, span].astype(F32) + bt[1, span].astype(F32) + in_bt[2, span].astype(F32)
-        input_grad_ref[0, 0, :, 128 * q : 128 * q + 128] = summed.astype(BF16)
+        input_grad_out[:, 128 * q : 128 * q + 128] = summed.astype(BF16)
+    outs.append(local(input_grad_out, input_grad_ref.at[0, 0], out_sem.at[1]))
+    outs[1].start()
 
     fw_copies = []
     for kind in range(2):
-        span = gath.at[core, pl.ds(per_kind * kind, per_kind)]
+        span = gath.at[core, pl.ds(blocks // 2 * kind, blocks // 2)]
         local(span, span, ag_recv.at[kind]).wait()
         cp = remote(span, span, fw_send.at[kind], fw_recv.at[kind], r.partner)
         cp.start()
@@ -388,34 +399,56 @@
         far_halo.wait_send()
 
     for is_me, cp in rs_copies:
-
-        @pl.when(jnp.logical_not(is_me))
-        def _(cp=cp):
-            cp.wait_send()
-
-    for cp in fw_copies:
+        unless(is_me, cp.wait_send)
+    for kind in range(2):
+        fw_copies[kind].wait()
+        first, last = blocks // 2 * kind, min(blocks // 2 * (kind + 1), taps)
+        for h in range(2):
+            value = gath[h, first:last].astype(F32) * (1.0 / loss_scale)
+            weights[first:last, 32 * h : 32 * h + 32, :] = value
+        span = pl.ds(first, last - first)
+        outs.append(local(weights.at[span], weight_grad_ref.at[span], out_sem.at[2 + kind]))
+        outs[-1].start()
+    bias_out[...] = gath[0, taps, 0, :].astype(F32) * (1.0 / loss_scale)
+    outs.append(local(bias_out, bias_grad_ref, out_sem.at[4]))
+    outs[-1].start()
+    for cp in outs:
         cp.wait()
-    for h in range(2):
-        total_ref[:, 32 * h : 32 * h + 32, :] = gath[h].astype(F32) * (1.0 / loss_scale)
+
+
+def hand_over(pooled, input_grad, weight_grad, bias_grad, pooled_ref, input_grad_ref, weight_ref, bias_ref, w, g, p, b, get, put):
+    moves = [(weight_grad.at[pl.ds(9 * i, 9)], w.at[pl.ds(9 * i, 9)], weight_ref.at[pl.ds(9 * i, 9)]) for i in range(3)]
+    moves += [(input_grad, g, input_grad_ref), (pooled, p, pooled_ref), (bias_grad, b, bias_ref)]
+    reads = [local(src, mid, get.at[i]) for i, (src, mid, dst) in enumerate(moves)]
+    writes = [local(mid, dst, put.at[i]) for i, (src, mid, dst) in enumerate(moves)]
+    for cp in reads:
+        cp.start()
+    for arrive, leave in zip(reads, writes):
+        arrive.wait()
+        leave.start()
+    for cp in writes:
+        cp.wait()
 
 
 def block(volume, weight, conv_bias, cotangent):
     dma = pltpu.SemaphoreType.DMA
     vmem = pltpu.VMEM
-    anywhere = pl.BlockSpec(memory_space=pl.ANY)
-    here = pl.BlockSpec(memory_space=pltpu.VMEM)
-    pooled, input_grad, total = pl.pallas_call(
+    anywhere = pl.BlockSpec(memory_space=pltpu.HBM)
+    shapes = (
+        jax.ShapeDtypeStruct(cotangent.shape, BF16),
+        jax.ShapeDtypeStruct(volume.shape, BF16),
+        jax.ShapeDtypeStruct((taps, 64, 128), F32),
+        jax.ShapeDtypeStruct(conv_bias.shape, F32),
+    )
+    results = pl.pallas_call(
         block_kernel,
-        out_shape=(
-            jax.ShapeDtypeStruct(cotangent.shape, BF16),
-            jax.ShapeDtypeStruct(volume.shape, BF16),
-            jax.ShapeDtypeStruct((pieces, 64, 128), F32),
-        ),
-        in_specs=[anywhere, anywhere, here, anywhere],
-        out_specs=(here, here, here),
+        out_shape=shapes,
+        in_specs=[anywhere, anywhere, anywhere, anywhere],
+        out_specs=(anywhere,) * 4,
         scratch_shapes=[
             vmem((3, side, 2304), BF16),
             vmem((3, 3, 3, 64, 128), BF16),
+            vmem((128,), F32),
             vmem((2, 8, 16, 128), BF16),
             vmem((3, 768, 256), BF16),
             vmem((3, 384, 512), BF16),
@@ -433,26 +466,39 @@
             vmem((cells, 128), F32),
             vmem((cells, 128), F32),
             vmem((3, cells + 2 * side, 256), BF16),
-            vmem((pieces, 64, 128), F32),
+            vmem((blocks, 64, 128), F32),
             vmem((3, cells, 128), BF16),
             vmem((3, cells, 128), BF16),
-            vmem((pieces, 32, 128), BF16),
-            vmem((pieces, 32, 128), BF16),
-            vmem((pieces, 32, 128), BF16),
-            vmem((32, 32, 128), BF16),
-            vmem((32, 128), BF16),
-            vmem((8, 32, 128), BF16),
-            vmem((32, 128), BF16),
-            vmem((2, pieces, 32, 128), BF16),
-            dma((3,)), dma((2,)), dma((2,)), dma, dma, dma((4,)), dma((4,)), dma((2,)), dma((2,)),
-            dma((9,)), dma((9,)), dma((pieces,)), dma, dma((8,)), dma, dma((31,)), dma((2,)), dma((2,)), dma((2,)),
+            vmem((blocks, 32, 128), BF16),
+            vmem((blocks, 32, 128), BF16),
+            vmem((blocks, 32, 128), BF16),
+            vmem((32, per_piece, 32, 128), BF16),
+            vmem((per_piece, 32, 128), BF16),
+            vmem((8, per_piece, 32, 128), BF16),
+            vmem((per_piece, 32, 128), BF16),
+            vmem((2, blocks, 32, 128), BF16),
+            vmem((8, 16, 128), BF16),
+            vmem((side, 2048), BF16),
+            vmem((taps, 64, 128), F32),
+            vmem((128,), F32),
+            dma((4,)), dma((2,)), dma((2,)), dma, dma, dma((4,)), dma((4,)), dma((2,)), dma((2,)),
+            dma((9,)), dma((9,)), dma((pieces,)), dma, dma((8,)), dma, dma((32,)), dma((2,)), dma((2,)), dma((2,)), dma((6,)),
         ],
         compiler_params=pltpu.CompilerParams(
-            collective_id=0, has_side_effects=True, vmem_limit_bytes=48 * 2**20
+            collective_id=0, has_side_effects=True, vmem_limit_bytes=62 * 2**20
         ),
         name="conv_block",
     )(volume, weight, conv_bias, cotangent)
-    return pooled, input_grad, total[:taps].reshape(weight.shape), total[taps, 0]
+    pooled, input_grad, weight_grad, bias_grad = pl.pallas_call(
+        hand_over,
+        out_shape=shapes,
+        in_specs=[anywhere] * 4,
+        out_specs=(anywhere,) * 4,
+        scratch_shapes=[vmem(v.shape, v.dtype) for v in (shapes[2], shapes[1], shapes[0], shapes[3])] + [dma((6,)), dma((6,))],
+        compiler_params=pltpu.CompilerParams(vmem_limit_bytes=62 * 2**20),
+        name="hand_over",
+    )(*results)
+    return pooled, input_grad, weight_grad.reshape(weight.shape), bias_grad
 
 
 def solution(mesh):

time: 56.3 us -> 51.3 us (0.911)
  local copies, waits for them, and re-layouts: 6.07 us -> 0 us
  Pallas kernels: 49.3 us -> 50.5 us
    unnamed x10 -> x0, local copies, waits for them, and re-layouts: 4.59 us -> none
    pallas_call x1 -> x2, Pallas kernels: 49.3 us -> 50.5 us  [the longest x1 48.5 us: block(): pl.pallas_call(block_kernel, out_shape=shapes, in_specs=[anywhere, anywhe...]
    slice x1 -> x0, local copies, waits for them, and re-layouts: 0.97 us -> none  [block(): total[:taps].reshape(weight.shape)]
where the time goes in v3:
time: 51.3 us; the launch traced here: 51.1 us
  Pallas kernels  50.5 us (98%)
  between operations  0.64 us (1%)
    pallas_call x1, Pallas kernels, block(): pl.pallas_call(block_kernel, out_shape=shapes, in_specs=[anywhere, anywhe...  48.5 us
    pallas_call x1, Pallas kernels, block(): pl.pallas_call(hand_over, out_shape=shapes, in_specs=[anywhere] * 4, out_...  2.02 us

profile of v3, /device:TPU:1, one launch (start us, length us, event | category | flops | bytes accessed | tf_op | source)
XLA Modules:
  0.0 51.1 jit_solution(13404838060183866863)
XLA Ops:
  0.6 48.5 %conv_block.1 = (bf16[1,8,16,128]{3,2,1,0:T(8,128)(2,1)}, bf16[1,1,32,2048]{3,2,1,0:T(8,128)(2,1)}, f32[27,64,128]{2,1,0:T(8,128)}, f32[128]{0:T(128)}) custom-call(bf16[1,1,32,2048]{3,2,1,0:T(8,128)(2,1)} %volume_ref.1, bf16[3,3,3,64,128]{4,3,2,1,0:T(8,128)(2,1)} %weight_ref.1, f32[128]{0:T(128)} %bias_hbm.1, bf16[1,8,16,128]{3,2,1,0:T(8,128)(2,1)} %cot_ref.1), custom_call_target="tpu_custom_call" | custom-call | tf_op jit(solution)/shard_map/conv_block/pallas_call | solution.py:443
  49.1 2.0 %hand_over.1 = (bf16[1,8,16,128]{3,2,1,0:T(8,128)(2,1)}, bf16[1,1,32,2048]{3,2,1,0:T(8,128)(2,1)}, f32[27,64,128]{2,1,0:T(8,128)}, f32[128]{0:T(128)}) custom-call(bf16[1,8,16,128]{3,2,1,0:T(8,128)(2,1)} %get-tuple-element.12.pooled, bf16[1,1,32,2048]{3,2,1,0:T(8,128)(2,1)} %get-tuple-element.13.input_grad, f32[27,64,128]{2,1,0:T(8,128)} %get-tuple-element.14.weight_grad, ...), custom_call_target="tpu_custom_call" | custom-call | tf_op jit(solution)/shard_map/hand_over/pallas_call | solution.py:492

commit v4 on v3

--- a/solution.py
+++ b/solution.py
@@ -17,7 +17,6 @@
 pairs = 16
 cells = 512
 loss_scale = 256.0
-plane_order = sorted(((x, row) for x in range(4) for row in range(8)), key=sum)
 spots = tuple((x, row) for row in range(7) for x in range(2))
 
 
@@ -61,15 +60,18 @@
         self.near_tap = 2 - 2 * self.core
         self.far_tap = 2 * self.core
 
-    def plane_peer(self, x, row):
+    def plane_peer(self, i):
+        at = i + jnp.where(i >= self.row_at * 4 + self.x, 1, 0)
+        row = lax.div(at, 4)
         y = jnp.where(self.kind_a, row, self.y)
         z = jnp.where(self.kind_a, self.z, row)
-        return ident(x, y, z, self.core), jnp.logical_and(self.x == x, self.row_at == row)
-
-    def ring_peer(self, at):
+        return ident(lax.rem(at, 4), y, z, self.core)
+
+    def ring_peer(self, i):
+        at = i + jnp.where(i >= self.ring_at, 1, 0)
         y = jnp.where(self.kind_a, self.y, at)
         z = jnp.where(self.kind_a, at, self.z)
-        return ident(self.x, y, z, self.core), self.ring_at == at
+        return ident(self.x, y, z, self.core)
 
     def owner_of(self, piece):
         kind, i = divmod(piece, per_kind)
@@ -113,12 +115,12 @@
                     wb[b, at : at + 64, 128 * j : 128 * j + 128] = block
 
 
-def lay_plane(xin, xk, p):
+def lay_plane(xin, xk, p, chunks=range(4)):
     width = 512
     row = lax.broadcasted_iota(jnp.int32, (side, width), 0)
     low = lax.rem(lax.broadcasted_iota(jnp.int32, (side, width), 1), 128) < 64
     first, last = row == 0, row == side - 1
-    for chunk in range(4):
+    for chunk in chunks:
         at = width * chunk
         left = xin[p, :, at : at + width].astype(F32)
         here = xin[p, :, at + 128 : at + 128 + width].astype(F32)
@@ -141,10 +143,10 @@
 
 def block_kernel(
     volume_ref, weight_ref, bias_hbm, cot_ref,
-    pooled_ref, input_grad_ref, weight_grad_ref, bias_grad_ref,
+    pooled_ref, input_grad_ref, sum_ref,
     xin, wraw, bias_ref, cots, wf, wb, xk, xt, pre, act, pe, sum_e, sum_n, sums, psums, ctab, pvt, fa, fb, gs, part, bt, in_bt,
     mine, theirs, rows, rs, ring_src, ring, final,
-    gath, pooled_out, input_grad_out, weights, bias_out,
+    gath, pooled_out, input_grad_out,
     load_sem, halo_send, halo_recv, cot_send, cot_recv, pool_send, pool_recv, bt_send, bt_recv,
     core_send, core_recv, rs_send, rs_recv, ring_send, ring_recv, ag_send, ag_recv, fw_send, fw_recv, out_sem,
 ):
@@ -170,12 +172,10 @@
 
     @pl.when(r.owner)
     def _():
-        for x, row in reversed(plane_order):
-            who, me = r.plane_peer(x, row)
-            unless(me, lambda who=who: signal(bar, who))
-        for at in range(8):
-            who, me = r.ring_peer(at)
-            unless(me, lambda who=who: signal(bar, who))
+        for i in reversed(range(31)):
+            signal(bar, r.plane_peer(i))
+        for i in range(7):
+            signal(bar, r.ring_peer(i))
 
     for p in range(3):
         xin[p, :, 0:128] = jnp.zeros((side, 128), BF16)
@@ -192,11 +192,15 @@
     pl.semaphore_wait(bar, pieces + 1 + 6 * own + jnp.where(r.far_exists, 1, 0))
 
     own_plane = xin.at[1, :, body_lanes]
-    far_halo = remote(own_plane, xin.at[2 - far, :, body_lanes], halo_send.at[0], halo_recv.at[0], r.far)
+    far_halos = []
+    for i, lanes in enumerate((pl.ds(128, 9 * 128), pl.ds(10 * 128, 7 * 128))):
+        src = xin.at[1, :, lanes]
+        far_halos.append(remote(src, xin.at[2 - far, :, lanes], halo_send.at[2 * i], halo_recv.at[2 * i], r.far))
 
     @pl.when(r.far_exists)
     def _():
-        far_halo.start()
+        for cp in far_halos:
+            cp.start()
 
     near_halo = remote(own_plane, xin.at[2 - near, :, body_lanes], halo_send.at[1], halo_recv.at[1], r.partner)
     near_halo.start()
@@ -213,8 +217,8 @@
     lay_plane(xin, xk, near)
     bias = bias_ref[...].reshape(1, 128)
     bias = jnp.concatenate([bias, bias], axis=1)
-    for m in range(4):
-        span = pl.ds(128 * m, 128)
+    for m in range(2):
+        span = pl.ds(256 * m, 256)
         pre[span] = (
             bias
             + jnp.dot(xk[1, span], wf[1], preferred_element_type=F32)
@@ -226,15 +230,15 @@
         for row in range(8):
             ctab[pl.ds(8 * half + row, 16, stride=16), :] = cots[half, row].astype(F32)
 
-    @pl.when(r.far_exists)
-    def _():
-        far_halo.wait_recv()
-
-    lay_plane(xin, xk, far)
     pool_copies = []
     for m in range(4):
+        if m % 2 == 0:
+            pl.when(r.far_exists)(far_halos[m // 2].wait_recv)
+            lay_plane(xin, xk, far, (m, m + 1))
+            both = pl.ds(128 * m, 256)
+            pre[both] = pre[both] + jnp.dot(xk[far, both], wf[far], preferred_element_type=F32)
         span = pl.ds(128 * m, 128)
-        v = pre[span] + jnp.dot(xk[far, span], wf[far], preferred_element_type=F32)
+        v = pre[span]
         s = 0.5 * jnp.tanh(0.5 * v) + 0.5
         z = v * s
         e = jnp.exp(z)
@@ -285,10 +289,27 @@
     core_copies = []
     part[27] = jnp.zeros((64, 128), F32)
     part[27, 0:1, :] = bias_part[:, :128] + bias_part[:, 128:]
-    for a in range(3):
-        for b in range(3):
-            g = a * 3 + b
-            block = jnp.dot(xt[a], gs[b, side : side + cells, :], preferred_element_type=F32)
+    rs_copies = []
+
+    def pass_on(g):
+        count = 3 if g < 8 else 4
+        span = pl.ds(3 * g, count)
+        core_copies[g].wait_recv()
+        rows[span] = (part[span, half, :] + theirs[span].astype(F32)).astype(BF16)
+        for piece in range(3 * g, 3 * g + count):
+            who, slot = r.owner_of(piece)
+            is_me = jnp.logical_and(r.owner, r.piece == piece)
+            taps_of = rows.at[pl.ds(piece, 1)]
+            cp = remote(taps_of, rs.at[slot], rs_send.at[piece], rs_recv, who)
+            unless(is_me, cp.start, local(taps_of, rs.at[r.slot], rs_recv).start)
+            rs_copies.append((is_me, cp))
+
+    turned = xt[...].reshape(768, cells)
+    for b in range(3):
+        stack = jnp.dot(turned, gs[b, side : side + cells, :], preferred_element_type=F32)
+        for a in range(3):
+            g = b * 3 + a
+            block = stack[256 * a : 256 * a + 256]
             part[3 * g] = block[192:256, :128] + block[0:64, 128:]
             part[3 * g + 1] = block[0:64, :128] + block[64:128, 128:]
             part[3 * g + 2] = block[64:128, :128] + block[128:192, 128:]
@@ -297,23 +318,11 @@
             cp = remote(mine.at[span], theirs.at[span], core_send.at[g], core_recv.at[g], r.partner)
             cp.start()
             core_copies.append(cp)
-    rs_copies = []
-    sent = 0
-    for g in range(9):
-        count = 3 if g < 8 else 4
-        span = pl.ds(3 * g, count)
-        core_copies[g].wait_recv()
-        rows[span] = (part[span, half, :] + theirs[span].astype(F32)).astype(BF16)
-        while sent < pieces and per_piece * (sent + 1) <= 3 * g + count:
-            who, slot = r.owner_of(sent)
-            is_me = jnp.logical_and(r.owner, r.piece == sent)
-            taps_of = rows.at[pl.ds(per_piece * sent, per_piece)]
-            cp = remote(taps_of, rs.at[slot], rs_send.at[sent], rs_recv, who)
-            keep = local(taps_of, rs.at[r.slot], rs_recv)
-            unless(is_me, cp.start, keep.start)
-            rs_copies.append((is_me, cp))
-            sent += 1
-
+        if b:
+            for g in range(3 * b - 3, 3 * b):
+                pass_on(g)
+    for g in range(6, 9):
+        pass_on(g)
     for m in range(4):
         at = 128 * m
         total = jnp.zeros((128, 384), F32)
@@ -351,25 +360,20 @@
         for i in range(1, 32):
             total = total + rs[i].astype(F32)
         ring_src[...] = total.astype(BF16)
-        ring_copies = []
-        for at in range(8):
-            who, me = r.ring_peer(at)
-            cp = remote(ring_src, ring.at[r.ring_at], ring_send.at[at], ring_recv, who)
-            unless(me, cp.start, local(ring_src, ring.at[r.ring_at], ring_recv).start)
-            ring_copies.append((me, cp))
+        for i in range(7):
+            cp = remote(ring_src, ring.at[r.ring_at], ring_send.at[i], ring_recv, r.ring_peer(i))
+            cp.start()
+        local(ring_src, ring.at[r.ring_at], ring_recv).start()
         local(ring, ring, ring_recv).wait()
         total = ring[0].astype(F32)
         for i in range(1, 8):
             total = total + ring[i].astype(F32)
         final[...] = total.astype(BF16)
         place_of = gath.at[core, pl.ds(per_piece * r.piece, per_piece)]
-        for i, (x, row) in enumerate(plane_order):
-            who, me = r.plane_peer(x, row)
-            cp = remote(final, place_of, ag_send.at[i], ag_recv.at[r.kind], who)
-            unless(me, cp.start, local(final, place_of, ag_recv.at[r.kind]).start)
-            ring_copies.append((me, cp))
-        for me, cp in ring_copies:
-            unless(me, cp.wait_send)
+        for i in range(31):
+            cp = remote(final, place_of, ag_send.at[i], ag_recv.at[lax.div(r.piece, 7)], r.plane_peer(i))
+            cp.start()
+        local(final, place_of, ag_recv.at[lax.div(r.piece, 7)]).start()
 
     bt_near.wait()
 
@@ -385,47 +389,67 @@
     outs[1].start()
 
     fw_copies = []
-    for kind in range(2):
-        span = gath.at[core, pl.ds(blocks // 2 * kind, blocks // 2)]
+    for kind in range(4):
+        span = gath.at[core, pl.ds(7 * kind, 7)]
         local(span, span, ag_recv.at[kind]).wait()
         cp = remote(span, span, fw_send.at[kind], fw_recv.at[kind], r.partner)
         cp.start()
+        outs.append(local(span, sum_ref.at[core, pl.ds(7 * kind, 7)], out_sem.at[2 + kind]))
+        outs[-1].start()
         fw_copies.append(cp)
+    for kind in range(4):
+        fw_copies[kind].wait()
+        span = pl.ds(7 * kind, 7)
+        outs.append(local(gath.at[1 - core, span], sum_ref.at[1 - core, span], out_sem.at[6 + kind]))
+        outs[-1].start()
     for cp in core_copies + pool_copies + [near_halo, cot_copy]:
         cp.wait_send()
 
     @pl.when(r.far_exists)
     def _():
-        far_halo.wait_send()
+        for cp in far_halos:
+            cp.wait_send()
 
     for is_me, cp in rs_copies:
         unless(is_me, cp.wait_send)
-    for kind in range(2):
-        fw_copies[kind].wait()
-        first, last = blocks // 2 * kind, min(blocks // 2 * (kind + 1), taps)
-        for h in range(2):
-            value = gath[h, first:last].astype(F32) * (1.0 / loss_scale)
-            weights[first:last, 32 * h : 32 * h + 32, :] = value
-        span = pl.ds(first, last - first)
-        outs.append(local(weights.at[span], weight_grad_ref.at[span], out_sem.at[2 + kind]))
-        outs[-1].start()
-    bias_out[...] = gath[0, taps, 0, :].astype(F32) * (1.0 / loss_scale)
-    outs.append(local(bias_out, bias_grad_ref, out_sem.at[4]))
-    outs[-1].start()
+
+    @pl.when(r.owner)
+    def _():
+        for i in range(7):
+            local(ring_src, ring_src, ring_send.at[i]).wait()
+        for i in range(31):
+            local(final, final, ag_send.at[i]).wait()
+
     for cp in outs:
         cp.wait()
 
 
-def hand_over(pooled, input_grad, weight_grad, bias_grad, pooled_ref, input_grad_ref, weight_ref, bias_ref, w, g, p, b, get, put):
-    moves = [(weight_grad.at[pl.ds(9 * i, 9)], w.at[pl.ds(9 * i, 9)], weight_ref.at[pl.ds(9 * i, 9)]) for i in range(3)]
-    moves += [(input_grad, g, input_grad_ref), (pooled, p, pooled_ref), (bias_grad, b, bias_ref)]
-    reads = [local(src, mid, get.at[i]) for i, (src, mid, dst) in enumerate(moves)]
-    writes = [local(mid, dst, put.at[i]) for i, (src, mid, dst) in enumerate(moves)]
+def hand_over(
+    pooled, input_grad, total, pooled_ref, input_grad_ref, weight_ref, bias_ref, t, g, p, w, bias, get, put
+):
+    groups = (pl.ds(0, 9), pl.ds(9, 9), pl.ds(18, 10))
+    reads = [local(total.at[:, span], t.at[:, span], get.at[i]) for i, span in enumerate(groups)]
+    reads += [local(input_grad, g, get.at[3]), local(pooled, p, get.at[4])]
     for cp in reads:
         cp.start()
-    for arrive, leave in zip(reads, writes):
-        arrive.wait()
-        leave.start()
+    writes = []
+    for b in range(3):
+        reads[b].wait()
+        for a in range(3):
+            first, at = 9 * b + 3 * a, 9 * a + 3 * b
+            for h in range(2):
+                w[at : at + 3, 32 * h : 32 * h + 32, :] = t[h, first : first + 3].astype(F32) * (1.0 / loss_scale)
+            writes.append(local(w.at[pl.ds(at, 3)], weight_ref.at[pl.ds(at, 3)], put.at[3 * b + a]))
+            writes[-1].start()
+    bias[...] = t[0, taps, 0, :].astype(F32) * (1.0 / loss_scale)
+    writes.append(local(bias, bias_ref, put.at[9]))
+    writes[-1].start()
+    reads[3].wait()
+    writes.append(local(g, input_grad_ref, put.at[10]))
+    writes[-1].start()
+    reads[4].wait()
+    writes.append(local(p, pooled_ref, put.at[11]))
+    writes[-1].start()
     for cp in writes:
         cp.wait()
 
@@ -440,11 +464,12 @@
         jax.ShapeDtypeStruct((taps, 64, 128), F32),
         jax.ShapeDtypeStruct(conv_bias.shape, F32),
     )
+    sums = jax.ShapeDtypeStruct((2, blocks, 32, 128), BF16)
     results = pl.pallas_call(
         block_kernel,
-        out_shape=shapes,
-        in_specs=[anywhere, anywhere, anywhere, anywhere],
-        out_specs=(anywhere,) * 4,
+        out_shape=shapes[:2] + (sums,),
+        in_specs=[anywhere] * 4,
+        out_specs=(anywhere,) * 3,
         scratch_shapes=[
             vmem((3, side, 2304), BF16),
             vmem((3, 3, 3, 64, 128), BF16),
@@ -479,10 +504,8 @@
             vmem((2, blocks, 32, 128), BF16),
             vmem((8, 16, 128), BF16),
             vmem((side, 2048), BF16),
-            vmem((taps, 64, 128), F32),
-            vmem((128,), F32),
-            dma((4,)), dma((2,)), dma((2,)), dma, dma, dma((4,)), dma((4,)), dma((2,)), dma((2,)),
-            dma((9,)), dma((9,)), dma((pieces,)), dma, dma((8,)), dma, dma((32,)), dma((2,)), dma((2,)), dma((2,)), dma((6,)),
+            dma((4,)), dma((3,)), dma((3,)), dma, dma, dma((4,)), dma((4,)), dma((2,)), dma((2,)),
+            dma((9,)), dma((9,)), dma((pieces,)), dma, dma((8,)), dma, dma((32,)), dma((4,)), dma((4,)), dma((4,)), dma((10,)),
         ],
         compiler_params=pltpu.CompilerParams(
             collective_id=0, has_side_effects=True, vmem_limit_bytes=62 * 2**20
@@ -492,9 +515,10 @@
     pooled, input_grad, weight_grad, bias_grad = pl.pallas_call(
         hand_over,
         out_shape=shapes,
-        in_specs=[anywhere] * 4,
+        in_specs=[anywhere] * 3,
         out_specs=(anywhere,) * 4,
-        scratch_shapes=[vmem(v.shape, v.dtype) for v in (shapes[2], shapes[1], shapes[0], shapes[3])] + [dma((6,)), dma((6,))],
+        scratch_shapes=[vmem(v.shape, v.dtype) for v in (sums, shapes[1], shapes[0], shapes[2], shapes[3])]
+        + [dma((5,)), dma((12,))],
         compiler_params=pltpu.CompilerParams(vmem_limit_bytes=62 * 2**20),
         name="hand_over",
     )(*results)

time: 51.3 us -> 49.8 us (0.971)
  Pallas kernels: 50.5 us -> 49 us
    pallas_call x2, Pallas kernels: 50.5 us -> 49 us  [the longest x1 47 us: block(): pl.pallas_call(block_kernel, out_shape=shapes[:2] + (sums,), in_specs=[an...]
where the time goes in v4:
time: 49.8 us; the launch traced here: 49.6 us
  Pallas kernels  49 us (98%)
  between operations  0.64 us (1%)
    pallas_call x1, Pallas kernels, block(): pl.pallas_call(block_kernel, out_shape=shapes[:2] + (sums,), in_specs=[an...  47 us
    pallas_call x1, Pallas kernels, block(): pl.pallas_call(hand_over, out_shape=shapes, in_specs=[anywhere] * 3, out_...  2.02 us

profile of v4, /device:TPU:1, one launch (start us, length us, event | category | flops | bytes accessed | tf_op | source)
XLA Modules:
  0.0 49.6 jit_solution(13689887058148463665)
XLA Ops:
  0.6 47.0 %conv_block.1 = (bf16[1,8,16,128]{3,2,1,0:T(8,128)(2,1)}, bf16[1,1,32,2048]{3,2,1,0:T(8,128)(2,1)}, bf16[2,28,32,128]{3,2,1,0:T(8,128)(2,1)}) custom-call(bf16[1,1,32,2048]{3,2,1,0:T(8,128)(2,1)} %volume_ref.1, bf16[3,3,3,64,128]{4,3,2,1,0:T(8,128)(2,1)} %weight_ref.1, f32[128]{0:T(128)} %bias_hbm.1, bf16[1,8,16,128]{3,2,1,0:T(8,128)(2,1)} %cot_ref.1), custom_call_target="tpu_custom_call" | custom-call | tf_op jit(solution)/shard_map/conv_block/pallas_call | solution.py:468
  47.6 2.0 %hand_over.1 = (bf16[1,8,16,128]{3,2,1,0:T(8,128)(2,1)}, bf16[1,1,32,2048]{3,2,1,0:T(8,128)(2,1)}, f32[27,64,128]{2,1,0:T(8,128)}, f32[128]{0:T(128)}) custom-call(bf16[1,8,16,128]{3,2,1,0:T(8,128)(2,1)} %get-tuple-element.11.pooled, bf16[1,1,32,2048]{3,2,1,0:T(8,128)(2,1)} %get-tuple-element.12.input_grad, bf16[2,28,32,128]{3,2,1,0:T(8,128)(2,1)} %get-tuple-element.13.total), custom_call_target="tpu_custom_call" | custom-call | tf_op jit(solution)/shard_map/hand_over/pallas_call | solution.py:515

commit v5 on v4

--- a/solution.py
+++ b/solution.py
@@ -17,7 +17,7 @@
 pairs = 16
 cells = 512
 loss_scale = 256.0
-spots = tuple((x, row) for row in range(7) for x in range(2))
+spots = tuple((x, row) for row in (4, 3, 5, 2, 6, 1, 0) for x in (1, 0))
 
 
 def place():
@@ -50,7 +50,7 @@
             here = jnp.logical_and(side_x == sx, self.row_at == row)
             self.owner = jnp.logical_or(self.owner, here)
             self.piece = self.piece + jnp.where(here, i, 0)
-        self.piece = self.piece + self.kind * per_kind
+        self.piece = 2 * self.piece + self.kind
         self.slot = x * 8 + self.row_at
         self.partner = ident(x, y, z, 1 - self.core)
         plane = lax.axis_index("space")
@@ -74,7 +74,7 @@
         return ident(self.x, y, z, self.core)
 
     def owner_of(self, piece):
-        kind, i = divmod(piece, per_kind)
+        i, kind = divmod(piece, 2)
         x, row = spots[i]
         if kind == 0:
             return ident(x, row, self.z, self.core), self.x * 8 + self.y
@@ -369,7 +369,7 @@
         for i in range(1, 8):
             total = total + ring[i].astype(F32)
         final[...] = total.astype(BF16)
-        place_of = gath.at[core, pl.ds(per_piece * r.piece, per_piece)]
+        place_of = gath.at[pl.ds(per_piece * r.piece, per_piece)]
         for i in range(31):
             cp = remote(final, place_of, ag_send.at[i], ag_recv.at[lax.div(r.piece, 7)], r.plane_peer(i))
             cp.start()
@@ -390,18 +390,15 @@
 
     fw_copies = []
     for kind in range(4):
-        span = gath.at[core, pl.ds(7 * kind, 7)]
+        span = gath.at[pl.ds(7 * kind, 7)]
         local(span, span, ag_recv.at[kind]).wait()
-        cp = remote(span, span, fw_send.at[kind], fw_recv.at[kind], r.partner)
+        cp = remote(span, sum_ref.at[core, pl.ds(7 * kind, 7)], fw_send.at[kind], fw_recv.at[kind], r.partner)
         cp.start()
         outs.append(local(span, sum_ref.at[core, pl.ds(7 * kind, 7)], out_sem.at[2 + kind]))
         outs[-1].start()
         fw_copies.append(cp)
     for kind in range(4):
         fw_copies[kind].wait()
-        span = pl.ds(7 * kind, 7)
-        outs.append(local(gath.at[1 - core, span], sum_ref.at[1 - core, span], out_sem.at[6 + kind]))
-        outs[-1].start()
     for cp in core_copies + pool_copies + [near_halo, cot_copy]:
         cp.wait_send()
 
@@ -501,11 +498,11 @@
             vmem((per_piece, 32, 128), BF16),
             vmem((8, per_piece, 32, 128), BF16),
             vmem((per_piece, 32, 128), BF16),
-            vmem((2, blocks, 32, 128), BF16),
+            vmem((blocks, 32, 128), BF16),
             vmem((8, 16, 128), BF16),
             vmem((side, 2048), BF16),
             dma((4,)), dma((3,)), dma((3,)), dma, dma, dma((4,)), dma((4,)), dma((2,)), dma((2,)),
-            dma((9,)), dma((9,)), dma((pieces,)), dma, dma((8,)), dma, dma((32,)), dma((4,)), dma((4,)), dma((4,)), dma((10,)),
+            dma((9,)), dma((9,)), dma((pieces,)), dma, dma((8,)), dma, dma((32,)), dma((4,)), dma((4,)), dma((4,)), dma((6,)),
         ],
         compiler_params=pltpu.CompilerParams(
             collective_id=0, has_side_effects=True, vmem_limit_bytes=62 * 2**20

time: 49.8 us -> 47.4 us (0.952)
  Pallas kernels: 49 us -> 46.6 us
    pallas_call x1, Pallas kernels: 47 us -> 44.6 us  [block(): pl.pallas_call(block_kernel, out_shape=shapes[:2] + (sums,), in_specs=[an...]
where the time goes in v5:
time: 47.4 us; the launch traced here: 47.3 us
  Pallas kernels  46.6 us (98%)
  between operations  0.64 us (1%)
    pallas_call x1, Pallas kernels, block(): pl.pallas_call(block_kernel, out_shape=shapes[:2] + (sums,), in_specs=[an...  44.6 us
    pallas_call x1, Pallas kernels, block(): pl.pallas_call(hand_over, out_shape=shapes, in_specs=[anywhere] * 3, out_...  2.02 us

profile of v5, /device:TPU:1, one launch (start us, length us, event | category | flops | bytes accessed | tf_op | source)
XLA Modules:
  0.0 47.3 jit_solution(2694151095355121032)
XLA Ops:
  0.6 44.6 %conv_block.1 = (bf16[1,8,16,128]{3,2,1,0:T(8,128)(2,1)}, bf16[1,1,32,2048]{3,2,1,0:T(8,128)(2,1)}, bf16[2,28,32,128]{3,2,1,0:T(8,128)(2,1)}) custom-call(bf16[1,1,32,2048]{3,2,1,0:T(8,128)(2,1)} %volume_ref.1, bf16[3,3,3,64,128]{4,3,2,1,0:T(8,128)(2,1)} %weight_ref.1, f32[128]{0:T(128)} %bias_hbm.1, bf16[1,8,16,128]{3,2,1,0:T(8,128)(2,1)} %cot_ref.1), custom_call_target="tpu_custom_call" | custom-call | tf_op jit(solution)/shard_map/conv_block/pallas_call | solution.py:465
  45.3 2.0 %hand_over.1 = (bf16[1,8,16,128]{3,2,1,0:T(8,128)(2,1)}, bf16[1,1,32,2048]{3,2,1,0:T(8,128)(2,1)}, f32[27,64,128]{2,1,0:T(8,128)}, f32[128]{0:T(128)}) custom-call(bf16[1,8,16,128]{3,2,1,0:T(8,128)(2,1)} %get-tuple-element.11.pooled, bf16[1,1,32,2048]{3,2,1,0:T(8,128)(2,1)} %get-tuple-element.12.input_grad, bf16[2,28,32,128]{3,2,1,0:T(8,128)(2,1)} %get-tuple-element.13.total), custom_call_target="tpu_custom_call" | custom-call | tf_op jit(solution)/shard_map/hand_over/pallas_call | solution.py:512

commit v6 on v5

--- a/solution.py
+++ b/solution.py
@@ -340,14 +340,6 @@
             )
         for a in range(3):
             bt[a, at : at + 128, :] = total[:, 128 * a : 128 * a + 128].astype(BF16)
-    bt_far = remote(bt.at[far], in_bt.at[far], bt_send.at[0], bt_recv.at[0], r.far)
-
-    @pl.when(r.far_exists)
-    def _():
-        bt_far.start()
-
-    bt_near = remote(bt.at[near], in_bt.at[near], bt_send.at[1], bt_recv.at[1], r.partner)
-    bt_near.start()
     for row in range(8):
         pooled_out[row] = pvt[pl.ds(8 * core + row, 16, stride=16), :].astype(BF16)
 
@@ -364,6 +356,18 @@
             cp = remote(ring_src, ring.at[r.ring_at], ring_send.at[i], ring_recv, r.ring_peer(i))
             cp.start()
         local(ring_src, ring.at[r.ring_at], ring_recv).start()
+
+    bt_far = remote(bt.at[far], in_bt.at[far], bt_send.at[0], bt_recv.at[0], r.far)
+
+    @pl.when(r.far_exists)
+    def _():
+        bt_far.start()
+
+    bt_near = remote(bt.at[near], in_bt.at[near], bt_send.at[1], bt_recv.at[1], r.partner)
+    bt_near.start()
+
+    @pl.when(r.owner)
+    def _():
         local(ring, ring, ring_recv).wait()
         total = ring[0].astype(F32)
         for i in range(1, 8):

time: 47.4 us -> 47.4 us (level)
  no operation moved by 1% of the time
where the time goes in v6:
time: 47.4 us; the launch traced here: 47.2 us
  Pallas kernels  46.6 us (98%)
  between operations  0.64 us (1%)
    pallas_call x1, Pallas kernels, block(): pl.pallas_call(block_kernel, out_shape=shapes[:2] + (sums,), in_specs=[an...  44.5 us
    pallas_call x1, Pallas kernels, block(): pl.pallas_call(hand_over, out_shape=shapes, in_specs=[anywhere] * 3, out_...  2.02 us

profile of v6, /device:TPU:1, one launch (start us, length us, event | category | flops | bytes accessed | tf_op | source)
XLA Modules:
  0.0 47.2 jit_solution(7389852481421200294)
XLA Ops:
  0.6 44.5 %conv_block.1 = (bf16[1,8,16,128]{3,2,1,0:T(8,128)(2,1)}, bf16[1,1,32,2048]{3,2,1,0:T(8,128)(2,1)}, bf16[2,28,32,128]{3,2,1,0:T(8,128)(2,1)}) custom-call(bf16[1,1,32,2048]{3,2,1,0:T(8,128)(2,1)} %volume_ref.1, bf16[3,3,3,64,128]{4,3,2,1,0:T(8,128)(2,1)} %weight_ref.1, f32[128]{0:T(128)} %bias_hbm.1, bf16[1,8,16,128]{3,2,1,0:T(8,128)(2,1)} %cot_ref.1), custom_call_target="tpu_custom_call" | custom-call | tf_op jit(solution)/shard_map/conv_block/pallas_call | solution.py:469
  45.2 2.0 %hand_over.1 = (bf16[1,8,16,128]{3,2,1,0:T(8,128)(2,1)}, bf16[1,1,32,2048]{3,2,1,0:T(8,128)(2,1)}, f32[27,64,128]{2,1,0:T(8,128)}, f32[128]{0:T(128)}) custom-call(bf16[1,8,16,128]{3,2,1,0:T(8,128)(2,1)} %get-tuple-element.11.pooled, bf16[1,1,32,2048]{3,2,1,0:T(8,128)(2,1)} %get-tuple-element.12.input_grad, bf16[2,28,32,128]{3,2,1,0:T(8,128)(2,1)} %get-tuple-element.13.total), custom_call_target="tpu_custom_call" | custom-call | tf_op jit(solution)/shard_map/hand_over/pallas_call | solution.py:516

commit v7 on v6

--- a/solution.py
+++ b/solution.py
@@ -483,14 +483,14 @@
             vmem((cells, 256), F32),
             vmem((cells, 256), F32),
             vmem((cells, 256), F32),
-            vmem((cells, 128), F32),
-            vmem((cells, 128), F32),
+            vmem((cells + 8, 128), F32),
+            vmem((cells + 8, 128), F32),
             vmem((4, 2, 64, 128), F32),
             vmem((4, 2, 64, 128), F32),
-            vmem((256, 128), F32),
-            vmem((256, 128), F32),
-            vmem((cells, 128), F32),
-            vmem((cells, 128), F32),
+            vmem((272, 128), F32),
+            vmem((272, 128), F32),
+            vmem((cells + 8, 128), F32),
+            vmem((cells + 8, 128), F32),
             vmem((3, cells + 2 * side, 256), BF16),
             vmem((blocks, 64, 128), F32),
             vmem((3, cells, 128), BF16),

time: 47.4 us -> 47.4 us (level)
  no operation moved by 1% of the time
where the time goes in v7:
time: 47.4 us; the launch traced here: 47.2 us
  Pallas kernels  46.6 us (98%)
  between operations  0.64 us (1%)
    pallas_call x1, Pallas kernels, block(): pl.pallas_call(block_kernel, out_shape=shapes[:2] + (sums,), in_specs=[an...  44.5 us
    pallas_call x1, Pallas kernels, block(): pl.pallas_call(hand_over, out_shape=shapes, in_specs=[anywhere] * 3, out_...  2.02 us

profile of v7, /device:TPU:1, one launch (start us, length us, event | category | flops | bytes accessed | tf_op | source)
XLA Modules:
  0.0 47.2 jit_solution(2735407001296253076)
XLA Ops:
  0.6 44.5 %conv_block.1 = (bf16[1,8,16,128]{3,2,1,0:T(8,128)(2,1)}, bf16[1,1,32,2048]{3,2,1,0:T(8,128)(2,1)}, bf16[2,28,32,128]{3,2,1,0:T(8,128)(2,1)}) custom-call(bf16[1,1,32,2048]{3,2,1,0:T(8,128)(2,1)} %volume_ref.1, bf16[3,3,3,64,128]{4,3,2,1,0:T(8,128)(2,1)} %weight_ref.1, f32[128]{0:T(128)} %bias_hbm.1, bf16[1,8,16,128]{3,2,1,0:T(8,128)(2,1)} %cot_ref.1), custom_call_target="tpu_custom_call" | custom-call | tf_op jit(solution)/shard_map/conv_block/pallas_call | solution.py:469
  45.2 2.0 %hand_over.1 = (bf16[1,8,16,128]{3,2,1,0:T(8,128)(2,1)}, bf16[1,1,32,2048]{3,2,1,0:T(8,128)(2,1)}, f32[27,64,128]{2,1,0:T(8,128)}, f32[128]{0:T(128)}) custom-call(bf16[1,8,16,128]{3,2,1,0:T(8,128)(2,1)} %get-tuple-element.11.pooled, bf16[1,1,32,2048]{3,2,1,0:T(8,128)(2,1)} %get-tuple-element.12.input_grad, bf16[2,28,32,128]{3,2,1,0:T(8,128)(2,1)} %get-tuple-element.13.total), custom_call_target="tpu_custom_call" | custom-call | tf_op jit(solution)/shard_map/hand_over/pallas_call | solution.py:516

commit v8 on v7

--- a/solution.py
+++ b/solution.py
@@ -368,6 +368,7 @@
 
     @pl.when(r.owner)
     def _():
+        plane_peers = [r.plane_peer(i) for i in range(31)]
         local(ring, ring, ring_recv).wait()
         total = ring[0].astype(F32)
         for i in range(1, 8):
@@ -375,7 +376,7 @@
         final[...] = total.astype(BF16)
         place_of = gath.at[pl.ds(per_piece * r.piece, per_piece)]
         for i in range(31):
-            cp = remote(final, place_of, ag_send.at[i], ag_recv.at[lax.div(r.piece, 7)], r.plane_peer(i))
+            cp = remote(final, place_of, ag_send.at[i], ag_recv.at[lax.div(r.piece, 7)], plane_peers[i])
             cp.start()
         local(final, place_of, ag_recv.at[lax.div(r.piece, 7)]).start()
 

time: 47.4 us -> 47.4 us (level)
  no operation moved by 1% of the time
where the time goes in v8:
time: 47.4 us; the launch traced here: 47.2 us
  Pallas kernels  46.6 us (98%)
  between operations  0.64 us (1%)
    pallas_call x1, Pallas kernels, block(): pl.pallas_call(block_kernel, out_shape=shapes[:2] + (sums,), in_specs=[an...  44.6 us
    pallas_call x1, Pallas kernels, block(): pl.pallas_call(hand_over, out_shape=shapes, in_specs=[anywhere] * 3, out_...  2.02 us

profile of v8, /device:TPU:1, one launch (start us, length us, event | category | flops | bytes accessed | tf_op | source)
XLA Modules:
  0.0 47.2 jit_solution(4440457324062142017)
XLA Ops:
  0.6 44.6 %conv_block.1 = (bf16[1,8,16,128]{3,2,1,0:T(8,128)(2,1)}, bf16[1,1,32,2048]{3,2,1,0:T(8,128)(2,1)}, bf16[2,28,32,128]{3,2,1,0:T(8,128)(2,1)}) custom-call(bf16[1,1,32,2048]{3,2,1,0:T(8,128)(2,1)} %volume_ref.1, bf16[3,3,3,64,128]{4,3,2,1,0:T(8,128)(2,1)} %weight_ref.1, f32[128]{0:T(128)} %bias_hbm.1, bf16[1,8,16,128]{3,2,1,0:T(8,128)(2,1)} %cot_ref.1), custom_call_target="tpu_custom_call" | custom-call | tf_op jit(solution)/shard_map/conv_block/pallas_call | solution.py:470
  45.2 2.0 %hand_over.1 = (bf16[1,8,16,128]{3,2,1,0:T(8,128)(2,1)}, bf16[1,1,32,2048]{3,2,1,0:T(8,128)(2,1)}, f32[27,64,128]{2,1,0:T(8,128)}, f32[128]{0:T(128)}) custom-call(bf16[1,8,16,128]{3,2,1,0:T(8,128)(2,1)} %get-tuple-element.11.pooled, bf16[1,1,32,2048]{3,2,1,0:T(8,128)(2,1)} %get-tuple-element.12.input_grad, bf16[2,28,32,128]{3,2,1,0:T(8,128)(2,1)} %get-tuple-element.13.total), custom_call_target="tpu_custom_call" | custom-call | tf_op jit(solution)/shard_map/hand_over/pallas_call | solution.py:517
